TPU v7x, 256 devices: a whole 4x4x8 slice. The times are simulated.
256 devices in a mesh: band: 64 (over x, z, core), lev: 4 (over y).
Axes of the slice: x: 4, y: 4, z: 8, core: 2. Of those that a mesh axis runs over, the one named last changes fastest.
Arguments:
- fields: bfloat16 [8, 136, 65536], P(None, 'lev', 'band'), may hold values from -6 to 6
- depart: int32 [136, 65536], P('lev', 'band'), may hold values from -512 to -1
- fraction: bfloat16 [2, 136, 65536], P(None, 'lev', 'band'), may hold values from 0 to 1
- w_first: bfloat16 [8, 136, 256], replicated, may hold values from -0.1875 to 0.1875
- b_first: float32 [256], replicated, may hold values from -4 to 4
- w_middle: bfloat16 [256, 256], replicated, may hold values from -0.375 to 0.375
- b_middle: float32 [256], replicated, may hold values from -4 to 4
- w_last: bfloat16 [8, 136, 256], replicated, may hold values from -0.375 to 0.375
Outputs:
- updated: bfloat16 [8, 136, 65536], P(None, 'lev', 'band')
Inputs may be any that keep to these rules, and one draw needn't show every extreme that they name: The departure corner of arrival column c is column c + depart, counted around the cycle of 65536 columns.
All inputs are finite; a program needn't handle non-finite values.
Results may differ from a plain program's by a relative error of at most 0.0053.
Values may be sent and summed in bfloat16 or wider, within the bound.
A program may use at most 64 MiB of HBM per device.

v0:
```python
import math

import jax
import jax.numpy as jnp
from jax import lax
from jax.sharding import PartitionSpec as P

ROW = 512


def with_halo(shard, sides, width):
    for axis, dim in sides:
        peers, length = (lax.axis_size(axis), shard.shape[dim])
        up = [(i, (i + 1) % peers) for i in range(peers)]
        down = [(j, i) for i, j in up]
        last = lax.slice_in_dim(shard, length - width, length, axis=dim)
        first = lax.slice_in_dim(shard, 0, width, axis=dim)
        before = lax.ppermute(last, axis, up)
        after = lax.ppermute(first, axis, down)
        shard = jnp.concatenate([before, shard, after], axis=dim)
    return shard


def column_physics(block, w_first, b_first, w_middle, b_middle, w_last):
    first = (
        jnp.einsum("flh,flc->hc", w_first, block, preferred_element_type=jnp.float32)
        + b_first[:, None]
    )
    first = jax.nn.silu(first).astype(jnp.bfloat16)
    middle = jnp.dot(w_middle.T, first, preferred_element_type=jnp.float32) + b_middle[:, None]
    middle = jax.nn.silu(middle).astype(jnp.bfloat16)
    tendency = jnp.einsum("flh,hc->flc", w_last, middle, preferred_element_type=jnp.float32)
    return (block.astype(jnp.float32) + tendency).astype(jnp.bfloat16)


def on_device(fields, depart, fraction, w_first, b_first, w_middle, b_middle, w_last):
    nfield, nlev, ncols = fields.shape
    margin = ROW + 1
    extended = with_halo(fields, (("band", 2),), margin)
    block_cols = math.gcd(ncols, 128)
    nblocks = ncols // block_cols
    window = block_cols + ROW
    offsets = (0, 1, ROW, ROW + 1)

    def one_block(number):
        start = number * block_cols
        dep = lax.dynamic_slice_in_dim(depart, start, block_cols, 1)
        frac = lax.dynamic_slice_in_dim(fraction, start, block_cols, 2)
        local = jnp.arange(block_cols, dtype=jnp.int32)[None, :] + ROW + dep
        slots = jnp.arange(window, dtype=jnp.int32)
        onehot = (slots[None, :, None] == local[:, None, :]).astype(jnp.bfloat16)
        sources = jnp.stack(
            [lax.dynamic_slice_in_dim(extended, start + 1 + off, window, 2) for off in offsets],
            axis=1,
        )
        picks = jnp.einsum("fklw,lwb->fklb", sources, onehot, preferred_element_type=jnp.float32)
        along = frac[0].astype(jnp.float32)
        across = frac[1].astype(jnp.float32)
        weights = (
            (1.0 - along) * (1.0 - across),
            along * (1.0 - across),
            (1.0 - along) * across,
            along * across,
        )
        total = jnp.zeros((nfield, nlev, block_cols), jnp.float32)
        for which in range(4):
            total = total + weights[which][None] * picks[:, which]
        return total.astype(jnp.bfloat16)

    pieces = lax.map(one_block, jnp.arange(nblocks, dtype=jnp.int32))
    advected = pieces.transpose(1, 2, 0, 3).reshape(nfield, nlev, ncols)
    columns_view = lax.all_to_all(advected, "lev", split_axis=2, concat_axis=1, tiled=True)
    updated_cols = column_physics(columns_view, w_first, b_first, w_middle, b_middle, w_last)
    return lax.all_to_all(updated_cols, "lev", split_axis=1, concat_axis=2, tiled=True)


def solution(mesh):
    placed = (
        P(None, "lev", "band"),
        P("lev", "band"),
        P(None, "lev", "band"),
        P(),
        P(),
        P(),
        P(),
        P(),
    )
    return jax.shard_map(
        on_device, mesh=mesh, in_specs=placed, out_specs=P(None, "lev", "band"), check_vma=False
    )
```

profile of v0, /device:TPU:8, one launch (start us, length us, event | category | flops | bytes accessed | tf_op | source)
XLA Modules:
  0.0 123.8 jit_solution(11152390430750413491)
XLA Ops:
  0.0 1.3 %fusion.43 = (bf16[8,34,513]{2,0,1:T(8,128)(2,1)S(1)}, bf16[8,34,513]{2,0,1:T(8,128)(2,1)S(1)}) fusion(bf16[8,34,1024]{2,0,1:T(8,128)(2,1)} %param.10), kind=kLoop, calls=%fused_computation.59 | loop fusion | bytes 1116288 | tf_op jit(solution)/shard_map/slice | solution.py:17
  1.4 7.6 %collective-permute-start.1 = (bf16[8,34,513]{2,0,1:T(8,128)(2,1)S(1)}, bf16[8,34,513]{2,0,1:T(8,128)(2,1)S(1)}, u32[]{:S(2)}, u32[]{:S(2)}) collective-permute-start(bf16[8,34,513]{2,0,1:T(8,128)(2,1)S(1)} %get-tuple-element.187), channel_id=1, source_target_pairs={{4,0},{8,4},{12,8},{16,12},{20,16},{24,20},{28,24},{32,28},{36,32}... | collective-permute-start | bytes 837224 | tf_op jit(solution)/shard_map/ppermute | solution.py:19
  9.0 4.9 %collective-permute-done = bf16[8,34,513]{2,0,1:T(8,128)(2,1)S(1)} collective-permute-done((bf16[8,34,513]{2,0,1:T(8,128)(2,1)S(1)}, bf16[8,34,513]{2,0,1:T(8,128)(2,1)S(1)}, u32[]{:S(2)}, u32[]{:S(2)}) %collective-permute-start) | collective-permute-done | bytes 279104 | tf_op jit(solution)/shard_map/ppermute | solution.py:18
  13.9 2.7 %concatenate.3 = bf16[8,34,2050]{2,0,1:T(8,128)(2,1)S(1)} concatenate(bf16[8,34,513]{2,0,1:T(8,128)(2,1)S(1)} %collective-permute-done, bf16[8,34,1024]{2,0,1:T(8,128)(2,1)} %param.10, bf16[8,34,513]{2,0,1:T(8,128)(2,1)S(1)} %collective-permute-done.1), dimensions={2} | concatenate | bytes 2230400 | tf_op jit(solution)/shard_map/concatenate | solution.py:20
  16.6 64.8 %while.14 = (s32[]{:T(128)}, bf16[8,8,34,128]{3,1,2,0:T(8,128)(2,1)}, s32[8]{0:T(128)S(1)}, bf16[2,34,1024]{2,0,1:T(2,128)(2,1)}, s32[34,1024]{1,0:T(8,128)}, /*...) while((s32[]{:T(128)}, ...), condition=%wide.region_1.2_spmd, body=%wide.region_0.1_spmd.sunk | while | flops 186949008 | bytes 5642175 | solution.py:70
  17.8 1.4 %dynamic-slice_bitcast_fusion.5 = (bf16[8,1,34,640]{3,0,1,2:T(8,128)(2,1)S(1)}, bf16[8,1,34,640]{3,0,1,2:T(8,128)(2,1)S(1)}, bf16[8,1,34,640]{3,0,1,2:T(8,128)(2,1)S(1)}, bf16[8,1,34,640]{3,0,1,2:T(8,128)(2,1)}) fusion(bf16[8,34,2050]{2,0,1:T(8,128)(2,1)S(1)} %get-tuple-element.291, s32[]{:T(128)S(6)} %select_n.51, s32[]{:T(128)S(6)} %select_n.52, ...), kind=kLoop, calls=%fused_computation.15.clone.1 | loop fusion | bytes 2785296 | tf_op jit(solution)/shard_map/while/body/eval_jaxpr/stack | solution.py:52
  19.2 0.7 dynamic-slice_add_fusion.2
  19.9 3.2 %fusion.56 = f32[8,4,34,128]{3,0,1,2:T(8,128)S(1)} fusion(bf16[8,1,34,640]{3,0,1,2:T(8,128)(2,1)S(1)} %get-tuple-element.238, bf16[8,1,34,640]{3,0,1,2:T(8,128)(2,1)S(1)} %get-tuple-element.239, bf16[8,1,34,640]{3,0,1,2:T(8,128)(2,1)} %get-tuple-element.240, bf16[8,1,34,640]{3,0,1,2:T(8,128)(2,1)S(1)} %get-tuple-element.241, ...), kind=kOutput, calls=%fused_computation.11.clone.1 | convolution fusion | flops 186613760 | bytes 1967104 | tf_op jit(solution)/shard_map/while/body/eval_jaxpr/fklw,lwb->fklb/dot_general | solution.py:56
  23.1 0.9 constant_dynamic-slice_fusion.3
  24.0 0.7 fusion.59
  25.9 1.4 %dynamic-slice_bitcast_fusion.5 = (bf16[8,1,34,640]{3,0,1,2:T(8,128)(2,1)S(1)}, bf16[8,1,34,640]{3,0,1,2:T(8,128)(2,1)S(1)}, bf16[8,1,34,640]{3,0,1,2:T(8,128)(2,1)S(1)}, bf16[8,1,34,640]{3,0,1,2:T(8,128)(2,1)}) fusion(bf16[8,34,2050]{2,0,1:T(8,128)(2,1)S(1)} %get-tuple-element.291, s32[]{:T(128)S(6)} %select_n.51, s32[]{:T(128)S(6)} %select_n.52, ...), kind=kLoop, calls=%fused_computation.15.clone.1 | loop fusion | bytes 2785296 | tf_op jit(solution)/shard_map/while/body/eval_jaxpr/stack | solution.py:52
  27.3 0.7 dynamic-slice_add_fusion.2
  28.0 3.2 %fusion.56 = f32[8,4,34,128]{3,0,1,2:T(8,128)S(1)} fusion(bf16[8,1,34,640]{3,0,1,2:T(8,128)(2,1)S(1)} %get-tuple-element.238, bf16[8,1,34,640]{3,0,1,2:T(8,128)(2,1)S(1)} %get-tuple-element.239, bf16[8,1,34,640]{3,0,1,2:T(8,128)(2,1)} %get-tuple-element.240, bf16[8,1,34,640]{3,0,1,2:T(8,128)(2,1)S(1)} %get-tuple-element.241, ...), kind=kOutput, calls=%fused_computation.11.clone.1 | convolution fusion | flops 186613760 | bytes 1967104 | tf_op jit(solution)/shard_map/while/body/eval_jaxpr/fklw,lwb->fklb/dot_general | solution.py:56
  31.2 0.9 constant_dynamic-slice_fusion.3
  32.1 0.7 fusion.59
  34.0 1.4 %dynamic-slice_bitcast_fusion.5 = (bf16[8,1,34,640]{3,0,1,2:T(8,128)(2,1)S(1)}, bf16[8,1,34,640]{3,0,1,2:T(8,128)(2,1)S(1)}, bf16[8,1,34,640]{3,0,1,2:T(8,128)(2,1)S(1)}, bf16[8,1,34,640]{3,0,1,2:T(8,128)(2,1)}) fusion(bf16[8,34,2050]{2,0,1:T(8,128)(2,1)S(1)} %get-tuple-element.291, s32[]{:T(128)S(6)} %select_n.51, s32[]{:T(128)S(6)} %select_n.52, ...), kind=kLoop, calls=%fused_computation.15.clone.1 | loop fusion | bytes 2785296 | tf_op jit(solution)/shard_map/while/body/eval_jaxpr/stack | solution.py:52
  35.4 0.7 dynamic-slice_add_fusion.2
  36.1 3.2 %fusion.56 = f32[8,4,34,128]{3,0,1,2:T(8,128)S(1)} fusion(bf16[8,1,34,640]{3,0,1,2:T(8,128)(2,1)S(1)} %get-tuple-element.238, bf16[8,1,34,640]{3,0,1,2:T(8,128)(2,1)S(1)} %get-tuple-element.239, bf16[8,1,34,640]{3,0,1,2:T(8,128)(2,1)} %get-tuple-element.240, bf16[8,1,34,640]{3,0,1,2:T(8,128)(2,1)S(1)} %get-tuple-element.241, ...), kind=kOutput, calls=%fused_computation.11.clone.1 | convolution fusion | flops 186613760 | bytes 1967104 | tf_op jit(solution)/shard_map/while/body/eval_jaxpr/fklw,lwb->fklb/dot_general | solution.py:56
  39.3 0.9 constant_dynamic-slice_fusion.3
  40.2 0.7 fusion.59
  42.1 1.4 %dynamic-slice_bitcast_fusion.5 = (bf16[8,1,34,640]{3,0,1,2:T(8,128)(2,1)S(1)}, bf16[8,1,34,640]{3,0,1,2:T(8,128)(2,1)S(1)}, bf16[8,1,34,640]{3,0,1,2:T(8,128)(2,1)S(1)}, bf16[8,1,34,640]{3,0,1,2:T(8,128)(2,1)}) fusion(bf16[8,34,2050]{2,0,1:T(8,128)(2,1)S(1)} %get-tuple-element.291, s32[]{:T(128)S(6)} %select_n.51, s32[]{:T(128)S(6)} %select_n.52, ...), kind=kLoop, calls=%fused_computation.15.clone.1 | loop fusion | bytes 2785296 | tf_op jit(solution)/shard_map/while/body/eval_jaxpr/stack | solution.py:52
  43.5 0.7 dynamic-slice_add_fusion.2
  44.2 3.2 %fusion.56 = f32[8,4,34,128]{3,0,1,2:T(8,128)S(1)} fusion(bf16[8,1,34,640]{3,0,1,2:T(8,128)(2,1)S(1)} %get-tuple-element.238, bf16[8,1,34,640]{3,0,1,2:T(8,128)(2,1)S(1)} %get-tuple-element.239, bf16[8,1,34,640]{3,0,1,2:T(8,128)(2,1)} %get-tuple-element.240, bf16[8,1,34,640]{3,0,1,2:T(8,128)(2,1)S(1)} %get-tuple-element.241, ...), kind=kOutput, calls=%fused_computation.11.clone.1 | convolution fusion | flops 186613760 | bytes 1967104 | tf_op jit(solution)/shard_map/while/body/eval_jaxpr/fklw,lwb->fklb/dot_general | solution.py:56
  47.4 0.9 constant_dynamic-slice_fusion.3
  48.3 0.7 fusion.59
  50.2 1.4 %dynamic-slice_bitcast_fusion.5 = (bf16[8,1,34,640]{3,0,1,2:T(8,128)(2,1)S(1)}, bf16[8,1,34,640]{3,0,1,2:T(8,128)(2,1)S(1)}, bf16[8,1,34,640]{3,0,1,2:T(8,128)(2,1)S(1)}, bf16[8,1,34,640]{3,0,1,2:T(8,128)(2,1)}) fusion(bf16[8,34,2050]{2,0,1:T(8,128)(2,1)S(1)} %get-tuple-element.291, s32[]{:T(128)S(6)} %select_n.51, s32[]{:T(128)S(6)} %select_n.52, ...), kind=kLoop, calls=%fused_computation.15.clone.1 | loop fusion | bytes 2785296 | tf_op jit(solution)/shard_map/while/body/eval_jaxpr/stack | solution.py:52
  51.6 0.7 dynamic-slice_add_fusion.2
  52.3 3.2 %fusion.56 = f32[8,4,34,128]{3,0,1,2:T(8,128)S(1)} fusion(bf16[8,1,34,640]{3,0,1,2:T(8,128)(2,1)S(1)} %get-tuple-element.238, bf16[8,1,34,640]{3,0,1,2:T(8,128)(2,1)S(1)} %get-tuple-element.239, bf16[8,1,34,640]{3,0,1,2:T(8,128)(2,1)} %get-tuple-element.240, bf16[8,1,34,640]{3,0,1,2:T(8,128)(2,1)S(1)} %get-tuple-element.241, ...), kind=kOutput, calls=%fused_computation.11.clone.1 | convolution fusion | flops 186613760 | bytes 1967104 | tf_op jit(solution)/shard_map/while/body/eval_jaxpr/fklw,lwb->fklb/dot_general | solution.py:56
  55.5 0.9 constant_dynamic-slice_fusion.3
  58.3 1.4 %dynamic-slice_bitcast_fusion.5 = (bf16[8,1,34,640]{3,0,1,2:T(8,128)(2,1)S(1)}, bf16[8,1,34,640]{3,0,1,2:T(8,128)(2,1)S(1)}, bf16[8,1,34,640]{3,0,1,2:T(8,128)(2,1)S(1)}, bf16[8,1,34,640]{3,0,1,2:T(8,128)(2,1)}) fusion(bf16[8,34,2050]{2,0,1:T(8,128)(2,1)S(1)} %get-tuple-element.291, s32[]{:T(128)S(6)} %select_n.51, s32[]{:T(128)S(6)} %select_n.52, ...), kind=kLoop, calls=%fused_computation.15.clone.1 | loop fusion | bytes 2785296 | tf_op jit(solution)/shard_map/while/body/eval_jaxpr/stack | solution.py:52
  59.7 0.7 dynamic-slice_add_fusion.2
  60.4 3.2 %fusion.56 = f32[8,4,34,128]{3,0,1,2:T(8,128)S(1)} fusion(bf16[8,1,34,640]{3,0,1,2:T(8,128)(2,1)S(1)} %get-tuple-element.238, bf16[8,1,34,640]{3,0,1,2:T(8,128)(2,1)S(1)} %get-tuple-element.239, bf16[8,1,34,640]{3,0,1,2:T(8,128)(2,1)} %get-tuple-element.240, bf16[8,1,34,640]{3,0,1,2:T(8,128)(2,1)S(1)} %get-tuple-element.241, ...), kind=kOutput, calls=%fused_computation.11.clone.1 | convolution fusion | flops 186613760 | bytes 1967104 | tf_op jit(solution)/shard_map/while/body/eval_jaxpr/fklw,lwb->fklb/dot_general | solution.py:56
  63.6 0.9 constant_dynamic-slice_fusion.3
  66.4 1.4 %dynamic-slice_bitcast_fusion.5 = (bf16[8,1,34,640]{3,0,1,2:T(8,128)(2,1)S(1)}, bf16[8,1,34,640]{3,0,1,2:T(8,128)(2,1)S(1)}, bf16[8,1,34,640]{3,0,1,2:T(8,128)(2,1)S(1)}, bf16[8,1,34,640]{3,0,1,2:T(8,128)(2,1)}) fusion(bf16[8,34,2050]{2,0,1:T(8,128)(2,1)S(1)} %get-tuple-element.291, s32[]{:T(128)S(6)} %select_n.51, s32[]{:T(128)S(6)} %select_n.52, ...), kind=kLoop, calls=%fused_computation.15.clone.1 | loop fusion | bytes 2785296 | tf_op jit(solution)/shard_map/while/body/eval_jaxpr/stack | solution.py:52
  67.8 0.7 dynamic-slice_add_fusion.2
  68.5 3.2 %fusion.56 = f32[8,4,34,128]{3,0,1,2:T(8,128)S(1)} fusion(bf16[8,1,34,640]{3,0,1,2:T(8,128)(2,1)S(1)} %get-tuple-element.238, bf16[8,1,34,640]{3,0,1,2:T(8,128)(2,1)S(1)} %get-tuple-element.239, bf16[8,1,34,640]{3,0,1,2:T(8,128)(2,1)} %get-tuple-element.240, bf16[8,1,34,640]{3,0,1,2:T(8,128)(2,1)S(1)} %get-tuple-element.241, ...), kind=kOutput, calls=%fused_computation.11.clone.1 | convolution fusion | flops 186613760 | bytes 1967104 | tf_op jit(solution)/shard_map/while/body/eval_jaxpr/fklw,lwb->fklb/dot_general | solution.py:56
  71.7 0.9 constant_dynamic-slice_fusion.3
  74.5 1.4 %dynamic-slice_bitcast_fusion.5 = (bf16[8,1,34,640]{3,0,1,2:T(8,128)(2,1)S(1)}, bf16[8,1,34,640]{3,0,1,2:T(8,128)(2,1)S(1)}, bf16[8,1,34,640]{3,0,1,2:T(8,128)(2,1)S(1)}, bf16[8,1,34,640]{3,0,1,2:T(8,128)(2,1)}) fusion(bf16[8,34,2050]{2,0,1:T(8,128)(2,1)S(1)} %get-tuple-element.291, s32[]{:T(128)S(6)} %select_n.51, s32[]{:T(128)S(6)} %select_n.52, ...), kind=kLoop, calls=%fused_computation.15.clone.1 | loop fusion | bytes 2785296 | tf_op jit(solution)/shard_map/while/body/eval_jaxpr/stack | solution.py:52
  75.9 0.7 dynamic-slice_add_fusion.2
  76.6 3.2 %fusion.56 = f32[8,4,34,128]{3,0,1,2:T(8,128)S(1)} fusion(bf16[8,1,34,640]{3,0,1,2:T(8,128)(2,1)S(1)} %get-tuple-element.238, bf16[8,1,34,640]{3,0,1,2:T(8,128)(2,1)S(1)} %get-tuple-element.239, bf16[8,1,34,640]{3,0,1,2:T(8,128)(2,1)} %get-tuple-element.240, bf16[8,1,34,640]{3,0,1,2:T(8,128)(2,1)S(1)} %get-tuple-element.241, ...), kind=kOutput, calls=%fused_computation.11.clone.1 | convolution fusion | flops 186613760 | bytes 1967104 | tf_op jit(solution)/shard_map/while/body/eval_jaxpr/fklw,lwb->fklb/dot_general | solution.py:56
  79.8 0.9 constant_dynamic-slice_fusion.3
  81.4 3.1 %copy.64 = bf16[8,34,8,128]{1,0,3,2:T(8,128)(2,1)} copy(bf16[8,34,8,128]{3,0,1,2:T(8,128)(2,1)} %bitcast.140) | data formatting | bytes 1114112 | tf_op jit(solution)/shard_map/reshape | solution.py:71
  84.5 4.8 %reshape.93 = bf16[4,2,34816]{2,1,0:T(2,128)(2,1)S(1)} reshape(bf16[1024,8,34]{2,1,0:T(8,128)(2,1)} %bitcast.136) | data formatting | bytes 1114112
  89.3 11.5 %all_to_all.36 = bf16[4,2,34816]{2,1,0:T(2,128)(2,1)S(1)} all-to-all(bf16[4,2,34816]{2,1,0:T(2,128)(2,1)S(1)} %reshape.93), channel_id=1, replica_groups=mesh['band'=64,'lev'=4] {'lev'}, dimensions={0} | all-to-all | bytes 1114112 | tf_op jit(solution)/shard_map/all_to_all | solution.py:72
  100.8 6.5 %reshape.94 = bf16[1024,8,34]{2,1,0:T(8,128)(2,1)} reshape(bf16[4,2,34816]{2,1,0:T(2,128)(2,1)S(1)} %all_to_all.36) | data formatting | bytes 1114112
  107.3 3.3 %copy.65 = bf16[8,34,4,256]{3,2,0,1:T(4,128)(2,1)S(1)} copy(bf16[8,34,4,256]{1,0,3,2:T(8,128)(2,1)} %bitcast.137) | data formatting | bytes 1114112 | tf_op jit(solution)/shard_map/all_to_all | solution.py:72
  112.3 10.6 %all_to_all.37 = bf16[8,136,256]{2,0,1:T(8,128)(2,1)S(1)} all-to-all(bf16[8,136,256]{2,0,1:T(8,128)(2,1)S(1)} %copy.60), channel_id=1, replica_groups=mesh['band'=64,'lev'=4] {'lev'}, dimensions={1} | all-to-all | bytes 1114112 | tf_op jit(solution)/shard_map/all_to_all | solution.py:74
  122.9 0.9 copy.74
  (54 shorter events, 9.3 us)
Async XLA Ops:
  0.0 111.2 %copy-start = (bf16[8,136,256]{2,1,0:T(8,128)(2,1)S(1)}, bf16[8,136,256]{2,1,0:T(8,128)(2,1)}, u32[]{:S(2)}) copy-start(bf16[8,136,256]{2,1,0:T(8,128)(2,1)} %param.17) | copy-start | bytes 1671172
  1.3 12.5 %collective-permute-start = (bf16[8,34,513]{2,0,1:T(8,128)(2,1)S(1)}, bf16[8,34,513]{2,0,1:T(8,128)(2,1)S(1)}, u32[]{:S(2)}, u32[]{:S(2)}) collective-permute-start(bf16[8,34,513]{2,0,1:T(8,128)(2,1)S(1)} %get-tuple-element.188), channel_id=1, source_target_pairs={{0,4},{4,8},{8,12},{12,16},{16,20},{20,24},{24,28},{28,32},{32,36}... | collective-permute-start | bytes 837224 | tf_op jit(solution)/shard_map/ppermute | solution.py:18
  1.4 12.5 %collective-permute-start.1 = (bf16[8,34,513]{2,0,1:T(8,128)(2,1)S(1)}, bf16[8,34,513]{2,0,1:T(8,128)(2,1)S(1)}, u32[]{:S(2)}, u32[]{:S(2)}) collective-permute-start(bf16[8,34,513]{2,0,1:T(8,128)(2,1)S(1)} %get-tuple-element.187), channel_id=1, source_target_pairs={{4,0},{8,4},{12,8},{16,12},{20,16},{24,20},{28,24},{32,28},{36,32}... | collective-permute-start | bytes 837224 | tf_op jit(solution)/shard_map/ppermute | solution.py:19
  107.3 3.4 %copy-start.1 = (bf16[8,136,256]{2,1,0:T(8,128)(2,1)S(1)}, bf16[8,136,256]{2,1,0:T(8,128)(2,1)}, u32[]{:S(2)}) copy-start(bf16[8,136,256]{2,1,0:T(8,128)(2,1)} %param.13) | copy-start | bytes 1671172
  107.3 3.5 %copy-start.3 = (f32[256]{0:T(256)S(1)}, f32[256]{0:T(256)}, u32[]{:S(2)}) copy-start(f32[256]{0:T(256)} %param.14) | copy-start | bytes 3076
  110.7 0.9 copy-start.2
  110.7 0.9 copy-start.4
where the time goes:
time: 126 us; the launch traced here: 124 us
  local copies, waits for them, and re-layouts  46.2 us (37%)
  matrix products  26.2 us (21%)
  blocking collectives  22.1 us (18%)
  other arithmetic  11.7 us (9%)
  starting transfers between devices  7.65 us (6%)
  loops' own time  4.93 us (4%)
  waiting for transfers between devices  4.89 us (4%)
    dot_general x8, matrix products, one_block(): jnp.einsum('fklw,lwb->fklb', sources, onehot, preferred_element_type=jnp....  25.3 us
    unnamed x12, local copies, waits for them, and re-layouts  11.8 us
    all_to_all x1, blocking collectives, on_device(): lax.all_to_all(advected, 'lev', split_axis=2, concat_axis=1, tiled=True)  11.5 us
    another operation x8, local copies, waits for them, and re-layouts, one_block(): jnp.stack([lax.dynamic_slice_in_dim(extended, start + 1 + off, window, 2)...  11.1 us
    all_to_all x1, blocking collectives, on_device(): lax.all_to_all(updated_cols, 'lev', split_axis=1, concat_axis=2, tiled=True)  10.6 us
    ppermute x1, starting transfers between devices, with_halo(): after = lax.ppermute(first, axis, down)  7.57 us
    slice x8, local copies, waits for them, and re-layouts, one_block(): across = frac[1].astype(jnp.float32)  7.18 us
    add x16, other arithmetic, one_block(): local = jnp.arange(block_cols, dtype=jnp.int32)[None, :] + ROW + dep  5.87 us
  transfers between devices with their start and end apart: 2, of which 1 were waited for; matrix products, arithmetic and copies ran while one was open for 0% of the time, Pallas kernels for 0%

commit v1 on v0

v1 whole, which is shorter than its diff:
```python
import functools

import jax
import jax.numpy as jnp
from jax import lax
from jax.experimental import pallas as pl
from jax.experimental.pallas import tpu as pltpu
from jax.sharding import PartitionSpec as P

MESH = pl.DeviceIdType.MESH
F32, BF16 = jnp.float32, jnp.bfloat16
LANES = 128
ROW = 512

_PICK = lax.GatherDimensionNumbers(
    offset_dims=(),
    collapsed_slice_dims=(1,),
    start_index_map=(1,),
    operand_batching_dims=(0,),
    start_indices_batching_dims=(0,),
)


def lane_gather(x, lane):
    return lax.gather(
        x, lane[..., None], _PICK, (1, 1), mode=lax.GatherScatterMode.PROMISE_IN_BOUNDS
    )


def silu(v):
    return v / (1.0 + jnp.exp(-v))


def kernel(
    nband, nlev, fields, depart, fraction, w_first, w_last, w_middle, b_first, b_middle, out,
    ext, dep_v, frac_v, wf_v, wl_v, wm_v, bf_v, bm_v, p16, w00, w01, w10, w11,
    adv, w1t, w3, w2t, b1, b2, part, opp_tx, opp_rx, near_tx, near_rx, mid, out_v,
    load_sem, halo_send, halo_recv, opp_send, opp_recv, near_send, near_recv,
    mid_send, mid_recv, fwd_send, fwd_recv, store_sem,
):
    band, me = lax.axis_index("band"), lax.axis_index("lev")
    nrow = adv.shape[0]
    levels = nrow // 8
    core = lax.rem(band, 2)
    east, west = lax.rem(band + 1, nband), lax.rem(band + nband - 1, nband)
    up, down, far = lax.rem(me + 1, nlev), lax.rem(me + nlev - 1, nlev), lax.rem(me + 2, nlev)

    barrier = pltpu.get_barrier_semaphore()
    for peer in ({"band": east}, {"band": west}, {"lev": up}, {"lev": down}):
        pl.semaphore_signal(barrier, inc=1, device_id=peer, device_id_type=MESH)

    loads = [
        pltpu.make_async_copy(src, dst, load_sem.at[n])
        for n, (src, dst) in enumerate(
            (
                (depart, dep_v), (fraction, frac_v), (w_first, wf_v), (w_last, wl_v), (w_middle, wm_v),
                (b_first, bf_v), (b_middle, bm_v), (fields, ext.at[:, :, pl.ds(ROW, 2 * ROW)]),
            )
        )
    ]
    for load in loads:
        load.start()
    pl.semaphore_wait(barrier, 4)

    halos = []
    for i in range(4):
        for side, peer, src, dst in ((0, east, 7 - i, 3 - i), (1, west, i, 12 + i)):
            copy = pltpu.make_async_remote_copy(
                src_ref=fields.at[:, :, pl.ds(src * LANES, LANES)],
                dst_ref=ext.at[:, :, pl.ds(dst * LANES, LANES)],
                send_sem=halo_send.at[side, i],
                recv_sem=halo_recv.at[side, i],
                device_id={"band": peer},
                device_id_type=MESH,
            )
            copy.start()
            halos.append(copy)

    loads[0].wait()
    loads[1].wait()

    def prepare(i, carry):
        lane = lax.rem(lax.broadcasted_iota(jnp.int32, (8, 2 * ROW), 1), LANES) + ROW
        where, weights = [], []
        for j in range(2):
            level = 2 * i + j
            where.append(lane + jnp.broadcast_to(dep_v[pl.ds(level, 1), :], (8, 2 * ROW)))
            both = frac_v[level].astype(F32)
            a = jnp.broadcast_to(both[0:1], (8, 2 * ROW))
            b = jnp.broadcast_to(both[1:2], (8, 2 * ROW))
            weights.append(((1.0 - a) * (1.0 - b), a * (1.0 - b), (1.0 - a) * b, a * b))
        rows = pl.ds(pl.multiple_of(16 * i, 16), 16)
        p16[rows, :] = jnp.concatenate(where, axis=0).astype(jnp.int16)
        for ref, one, two in zip((w00, w01, w10, w11), *weights):
            ref[rows, :] = jnp.concatenate([one, two], axis=0)
        return carry

    lax.fori_loop(0, levels // 2, prepare, 0)

    for load in loads[2:7]:
        load.wait()
    total_rows = wf_v.shape[0]
    total_levels = total_rows // 8
    r = lax.broadcasted_iota(jnp.int32, (nrow, total_rows), 0)
    source = lax.rem(r, 8) * total_levels + me * levels + r // 8
    pick = jnp.where(lax.broadcasted_iota(jnp.int32, (nrow, total_rows), 1) == source, 1.0, 0.0).astype(BF16)
    w3[...] = jnp.dot(pick, wl_v[...], preferred_element_type=F32).astype(BF16)
    w1t[...] = jnp.dot(pick, wf_v[...], preferred_element_type=F32).T.astype(BF16)
    w2t[...] = wm_v[...].astype(F32).T.astype(BF16)
    b1[...] = jnp.broadcast_to(bf_v[...], (LANES, bf_v.shape[1])).T
    b2[...] = jnp.broadcast_to(bm_v[...], (LANES, bm_v.shape[1])).T
    loads[7].wait()

    def advect(block):
        base = pl.multiple_of(block * LANES, LANES)
        cols = pl.ds(base, LANES)

        def group(g, carry):
            rows = pl.ds(pl.multiple_of(16 * g, 16), 16)
            p = p16[rows, cols]
            tiles = [
                ext[pl.ds(2 * g, 2), :, pl.ds(base + LANES * t, LANES)].reshape(16, LANES) for t in range(9)
            ]
            total = None
            for off, near, beyond in ((0, w00, w10), (1, w01, w11)):
                q = p + jnp.int16(off)
                lane = q & jnp.int16(LANES - 1)
                masks = [q >= jnp.int16(LANES * j) for j in range(1, 5)]
                got = [lane_gather(t, lane) for t in tiles]
                for start, weight in ((0, near), (4, beyond)):
                    value = got[start]
                    for j in range(4):
                        value = jnp.where(masks[j], got[start + j + 1], value)
                    term = weight[rows, cols] * value.astype(F32)
                    total = term if total is None else total + term
            adv[rows, cols] = total.astype(BF16)
            return carry

        lax.fori_loop(0, nrow // 16, group, 0)
        return cols

    def block_of(half, i):
        right = (1 - core) if half == 0 else core
        return right, right * (4 + i) + (1 - right) * (3 - i)

    def forward(half, i):
        right, block = block_of(half, i)
        tile = right * (12 + i) + (1 - right) * (3 - i)
        pltpu.make_async_remote_copy(
            src_ref=fields.at[:, :, pl.ds(0, LANES)],
            dst_ref=ext.at[:, :, pl.ds(pl.multiple_of(tile * LANES, LANES), LANES)],
            send_sem=halo_send.at[right, i],
            recv_sem=halo_recv.at[right, i],
            device_id={"band": east},
            device_id_type=MESH,
        ).wait_recv()
        cols = advect(block)
        part[half, i] = jnp.dot(w1t[...], adv[:, cols], preferred_element_type=F32)

    def remote(src, dst, send, recv, peer):
        return pltpu.make_async_remote_copy(
            src_ref=src, dst_ref=dst, send_sem=send, recv_sem=recv, device_id={"lev": peer}, device_id_type=MESH
        )

    hidden = w1t.shape[0]
    top, bottom = pl.ds(0, hidden // 2), pl.ds(hidden // 2, hidden // 2)
    sent = []

    def send_far(half):
        opp_tx[half] = part[half, far].astype(BF16)
        for way, rows, peer in ((0, top, up), (1, bottom, down)):
            copy = remote(
                opp_tx.at[half, rows], opp_rx.at[half, way], opp_send.at[half, way], opp_recv.at[half, way], peer
            )
            copy.start()
            sent.append(copy)

    def send_near(half):
        for way, rows, other, peer in ((0, top, bottom, up), (1, bottom, top, down)):
            remote(
                opp_tx.at[half, rows], opp_rx.at[half, way], opp_send.at[half, way], opp_recv.at[half, way], peer
            ).wait_recv()
            near_tx[half, way, rows] = (part[half, peer, rows] + opp_rx[half, way].astype(F32)).astype(BF16)
            near_tx[half, way, other] = part[half, peer, other].astype(BF16)
            copy = remote(
                near_tx.at[half, way], near_rx.at[half, way], near_send.at[half, way], near_recv.at[half, way], peer
            )
            copy.start()
            sent.append(copy)

    def finish(half):
        total = part[half, me] + b1[...]
        for way, peer in ((0, up), (1, down)):
            remote(
                near_tx.at[half, way], near_rx.at[half, way], near_send.at[half, way], near_recv.at[half, way], peer
            ).wait_recv()
            total = total + near_rx[half, way].astype(F32)
        first = silu(total).astype(BF16)
        second = jnp.dot(w2t[...], first, preferred_element_type=F32) + b2[...]
        mid[half, me] = silu(second).astype(BF16)
        for way, peer in ((0, up), (1, down)):
            copy = remote(
                mid.at[half, me], mid.at[half, me], mid_send.at[half, way], mid_recv.at[half, way], peer
            )
            copy.start()
            sent.append(copy)

    def pass_on(half):
        for way, rows, owner, peer in ((0, top, down, up), (1, bottom, up, down)):
            remote(
                mid.at[half, owner], mid.at[half, owner], mid_send.at[half, way], mid_recv.at[half, way], peer
            ).wait_recv()
            copy = remote(
                mid.at[half, owner, rows], mid.at[half, owner, rows],
                fwd_send.at[half, way], fwd_recv.at[half, way], peer,
            )
            copy.start()
            sent.append(copy)

    stores = []

    def last(half, i):
        _, block = block_of(half, i)
        cols = pl.ds(pl.multiple_of(block * LANES, LANES), LANES)
        tendency = jnp.dot(w3[...], mid[half, i], preferred_element_type=F32)
        updated = (adv[:, cols].astype(F32) + tendency).astype(BF16)
        out_v[:, :, cols] = updated.reshape(levels, 8, LANES)
        store = pltpu.make_async_copy(out_v.at[:, :, cols], out.at[:, :, cols], store_sem.at[half, i])
        store.start()
        stores.append(store)

    def finale(half):
        last(half, me)
        last(half, up)
        last(half, down)
        for way, rows, peer in ((0, top, up), (1, bottom, down)):
            remote(
                mid.at[half, far, rows], mid.at[half, far, rows],
                fwd_send.at[half, way], fwd_recv.at[half, way], peer,
            ).wait_recv()
        last(half, far)

    for i in range(4):
        forward(0, i)
    send_far(0)
    forward(1, 0)
    send_near(0)
    forward(1, 1)
    forward(1, 2)
    finish(0)
    forward(1, 3)
    send_far(1)
    pass_on(0)
    send_near(1)
    finale(0)
    finish(1)
    pass_on(1)
    finale(1)

    for copy in halos + sent:
        copy.wait_send()
    for store in stores:
        store.wait()


def on_device(nband, nlev, fields, depart, fraction, w_first, b_first, w_middle, b_middle, w_last):
    nfield, levels, ncols = fields.shape
    nrow, hidden = nfield * levels, w_middle.shape[0]
    V, DMA = pltpu.VMEM, pltpu.SemaphoreType.DMA
    table = V((nrow, ncols), F32)
    whole = V((nfield * w_first.shape[1], hidden), BF16)
    result = pl.pallas_call(
        functools.partial(kernel, nband, nlev),
        out_shape=jax.ShapeDtypeStruct((levels, nfield, ncols), BF16),
        in_specs=[pl.BlockSpec(memory_space=pl.ANY)] * 8,
        out_specs=pl.BlockSpec(memory_space=pl.ANY),
        scratch_shapes=[
            V((levels, nfield, 2 * ncols), BF16),
            V((levels, ncols), jnp.int32),
            V((levels, 2, ncols), BF16),
            whole,
            whole,
            V((hidden, hidden), BF16),
            V((1, hidden), F32),
            V((1, hidden), F32),
            V((nrow, ncols), jnp.int16),
            table, table, table, table,
            V((nrow, ncols), BF16),
            V((hidden, nrow), BF16),
            V((nrow, hidden), BF16),
            V((hidden, hidden), BF16),
            V((hidden, LANES), F32),
            V((hidden, LANES), F32),
            V((2, 4, hidden, LANES), F32),
            V((2, hidden, LANES), BF16),
            V((2, 2, hidden // 2, LANES), BF16),
            V((2, 2, hidden, LANES), BF16),
            V((2, 2, hidden, LANES), BF16),
            V((2, 4, hidden, LANES), BF16),
            V((levels, nfield, ncols), BF16),
            DMA((8,)), DMA((2, 4)), DMA((2, 4)), DMA((2, 2)), DMA((2, 2)), DMA((2, 2)), DMA((2, 2)),
            DMA((2, 2)), DMA((2, 2)), DMA((2, 2)), DMA((2, 2)), DMA((2, 4)),
        ],
        compiler_params=pltpu.CompilerParams(
            collective_id=0, has_side_effects=True, vmem_limit_bytes=40 << 20
        ),
    )(
        fields.transpose(1, 0, 2),
        depart,
        fraction.transpose(1, 0, 2),
        w_first.reshape(-1, hidden),
        w_last.reshape(-1, hidden),
        w_middle,
        b_first[None, :],
        b_middle[None, :],
    )
    return result.transpose(1, 0, 2)


def solution(mesh):
    placed = (P(None, "lev", "band"), P("lev", "band"), P(None, "lev", "band"), P(), P(), P(), P(), P())
    return jax.shard_map(
        functools.partial(on_device, mesh.shape["band"], mesh.shape["lev"]),
        mesh=mesh,
        in_specs=placed,
        out_specs=P(None, "lev", "band"),
        check_vma=False,
    )
```

time: 126 us -> 50.2 us (0.40); the launches traced: 124 us -> 49.9 us
  Pallas kernels: 0 us -> 42.5 us
  local copies, waits for them, and re-layouts: 46.2 us -> 7.38 us
  matrix products: 26.2 us -> 0 us
  blocking collectives: 22.1 us -> 0 us
  other arithmetic: 11.7 us -> 0 us
  starting transfers between devices: 7.65 us -> 0 us
  loops' own time: 4.93 us -> 0 us
  waiting for transfers between devices: 4.89 us -> 0 us
    pallas_call x0 -> x1, Pallas kernels: none -> 42.5 us  [on_device(): pl.pallas_call(functools.partial(kernel, nband, nlev), out_shape=jax.Shap...]
    dot_general x10 -> x0, matrix products: 26.2 us -> none  [the longest x8 25.3 us: one_block(): jnp.einsum('fklw,lwb->fklb', sources, onehot, preferred_element_type=jnp....]
    all_to_all x2 -> x0, blocking collectives: 22.1 us -> none  [the longest x1 11.5 us: on_device(): lax.all_to_all(advected, 'lev', split_axis=2, concat_axis=1, tiled=True)]
    another operation x8 -> x0, local copies, waits for them, and re-layouts: 11.1 us -> none  [one_block(): jnp.stack([lax.dynamic_slice_in_dim(extended, start + 1 + off, window, 2)...]
    slice x9 -> x0, local copies, waits for them, and re-layouts: 8.48 us -> none  [the longest x8 7.18 us: one_block(): across = frac[1].astype(jnp.float32)]
    ppermute x2 -> x0, starting transfers between devices: 7.65 us -> none  [the longest x1 7.57 us: with_halo(): after = lax.ppermute(first, axis, down)]
    add x16 -> x0, other arithmetic: 5.87 us -> none  [one_block(): local = jnp.arange(block_cols, dtype=jnp.int32)[None, :] + ROW + dep]
    dynamic_update_slice x8 -> x0, other arithmetic: 5.65 us -> none  [on_device(): pieces = lax.map(one_block, jnp.arange(nblocks, dtype=jnp.int32))]
  transfers between devices with their start and end apart: 2 -> 0, of which waited for: 1 -> 0; matrix products, arithmetic and copies ran while one was open for 0% -> 0% of each run, Pallas kernels for 0% -> 0%
where the time goes in v1:
time: 50.2 us; the launch traced here: 49.9 us
  Pallas kernels  42.5 us (85%)
  local copies, waits for them, and re-layouts  7.38 us (15%)
    pallas_call x1, Pallas kernels, on_device(): pl.pallas_call(functools.partial(kernel, nband, nlev), out_shape=jax.Shap...  42.5 us
    unnamed x17, local copies, waits for them, and re-layouts  7.38 us

profile of v1, /device:TPU:8, one launch (start us, length us, event | category | flops | bytes accessed | tf_op | source)
XLA Modules:
  0.0 49.9 jit_solution(6583929833546665364)
XLA Ops:
  0.0 0.0 copy-start.7
  0.0 0.0 copy-start.6
  0.0 0.7 %copy-done.7 = f32[256]{0:T(256)S(1)} copy-done((f32[256]{0:T(256)S(1)}, f32[256]{0:T(256)}, u32[]{:S(2)}) %copy-start.7) | copy-done | bytes 1048
  0.7 0.0 copy-done.6
  0.7 0.0 copy-start
  0.7 1.1 %copy-done = bf16[8,34,1024]{2,0,1:T(8,128)(2,1)S(1)} copy-done((bf16[8,34,1024]{2,0,1:T(8,128)(2,1)S(1)}, bf16[8,34,1024]{2,0,1:T(8,128)(2,1)}, u32[]{:S(2)}) %copy-start) | copy-done | bytes 557080
  1.7 0.0 copy-start.1
  1.8 1.1 %copy-done.1 = bf16[8,136,256]{2,1,0:T(8,128)(2,1)S(1)} copy-done((bf16[8,136,256]{2,1,0:T(8,128)(2,1)S(1)}, bf16[8,136,256]{2,1,0:T(8,128)(2,1)}, u32[]{:S(2)}) %copy-start.1) | copy-done | bytes 557080
  2.8 0.0 copy-start.2
  2.8 1.1 %copy-done.2 = bf16[8,136,256]{2,1,0:T(8,128)(2,1)S(1)} copy-done((bf16[8,136,256]{2,1,0:T(8,128)(2,1)S(1)}, bf16[8,136,256]{2,1,0:T(8,128)(2,1)}, u32[]{:S(2)}) %copy-start.2) | copy-done | bytes 557080
  3.9 0.0 copy-start.3
  3.9 0.9 %copy-done.3 = s32[34,1024]{1,0:T(8,128)S(1)} copy-done((s32[34,1024]{1,0:T(8,128)S(1)}, s32[34,1024]{1,0:T(8,128)}, u32[]{:S(2)}) %copy-start.3) | copy-done | bytes 139288
  4.8 0.0 copy-start.4
  4.8 0.9 %copy-done.4 = bf16[2,34,1024]{2,0,1:T(2,128)(2,1)S(1)} copy-done((bf16[2,34,1024]{2,0,1:T(2,128)(2,1)S(1)}, bf16[2,34,1024]{2,0,1:T(2,128)(2,1)}, u32[]{:S(2)}) %copy-start.4) | copy-done | bytes 139288
  5.7 0.0 copy-start.5
  5.7 0.9 %copy-done.5 = bf16[256,256]{1,0:T(8,128)(2,1)S(1)} copy-done((bf16[256,256]{1,0:T(8,128)(2,1)S(1)}, bf16[256,256]{1,0:T(8,128)(2,1)}, u32[]{:S(2)}) %copy-start.5) | copy-done | bytes 131096
  6.6 42.5 %shard_map.82 = bf16[34,8,1024]{2,1,0:T(8,128)(2,1)S(1)} custom-call(bf16[34,8,1024]{2,1,0:T(8,128)(2,1)S(1)} %bitcast.8, s32[34,1024]{1,0:T(8,128)S(1)} %copy-done.3, bf16[34,2,1024]{2,1,0:T(2,128)(2,1)S(1)} %bitcast.11, bf16[1088,256]{1,0:T(8,128)(2,1)S(1)} %bitcast.9, bf16[1088,256]{1,0:T(8,128)(2,1)S(1)} %bitcast.10, bf16[256,256]{1,0:T(8,128)(2,1)S(1)} %copy-done.5, ...), custom_call_target="tpu_custom_call" | custom-call | tf_op jit(solution)/shard_map/pallas_call | solution.py:272
  49.1 0.8 %copy.10 = bf16[8,34,1024]{2,0,1:T(8,128)(2,1)} copy(bf16[8,34,1024]{2,0,1:T(8,128)(2,1)S(1)} %bitcast.7) | data formatting | bytes 1114112
Async XLA Ops:
  0.0 0.7 %copy-start.7 = (f32[256]{0:T(256)S(1)}, f32[256]{0:T(256)}, u32[]{:S(2)}) copy-start(f32[256]{0:T(256)} %param.14) | copy-start | bytes 3076
  0.0 0.7 %copy-start.6 = (f32[256]{0:T(256)S(1)}, f32[256]{0:T(256)}, u32[]{:S(2)}) copy-start(f32[256]{0:T(256)} %param.12) | copy-start | bytes 3076
  0.7 1.1 %copy-start = (bf16[8,34,1024]{2,0,1:T(8,128)(2,1)S(1)}, bf16[8,34,1024]{2,0,1:T(8,128)(2,1)}, u32[]{:S(2)}) copy-start(bf16[8,34,1024]{2,0,1:T(8,128)(2,1)} %param.8) | copy-start | bytes 1671172
  1.7 1.1 %copy-start.1 = (bf16[8,136,256]{2,1,0:T(8,128)(2,1)S(1)}, bf16[8,136,256]{2,1,0:T(8,128)(2,1)}, u32[]{:S(2)}) copy-start(bf16[8,136,256]{2,1,0:T(8,128)(2,1)} %param.11) | copy-start | bytes 1671172
  2.8 1.1 %copy-start.2 = (bf16[8,136,256]{2,1,0:T(8,128)(2,1)S(1)}, bf16[8,136,256]{2,1,0:T(8,128)(2,1)}, u32[]{:S(2)}) copy-start(bf16[8,136,256]{2,1,0:T(8,128)(2,1)} %param.15) | copy-start | bytes 1671172
  3.9 0.9 %copy-start.3 = (s32[34,1024]{1,0:T(8,128)S(1)}, s32[34,1024]{1,0:T(8,128)}, u32[]{:S(2)}) copy-start(s32[34,1024]{1,0:T(8,128)} %depart.1) | copy-start | bytes 417796
  4.8 0.9 %copy-start.4 = (bf16[2,34,1024]{2,0,1:T(2,128)(2,1)S(1)}, bf16[2,34,1024]{2,0,1:T(2,128)(2,1)}, u32[]{:S(2)}) copy-start(bf16[2,34,1024]{2,0,1:T(2,128)(2,1)} %param.10) | copy-start | bytes 417796
  5.7 0.9 %copy-start.5 = (bf16[256,256]{1,0:T(8,128)(2,1)S(1)}, bf16[256,256]{1,0:T(8,128)(2,1)}, u32[]{:S(2)}) copy-start(bf16[256,256]{1,0:T(8,128)(2,1)} %w_middle.1) | copy-start | bytes 393220

commit v2 on v1

--- a/solution.py
+++ b/solution.py
@@ -102,7 +102,7 @@
     total_rows = wf_v.shape[0]
     total_levels = total_rows // 8
     r = lax.broadcasted_iota(jnp.int32, (nrow, total_rows), 0)
-    source = lax.rem(r, 8) * total_levels + me * levels + r // 8
+    source = (r & 7) * total_levels + me * levels + (r >> 3)
     pick = jnp.where(lax.broadcasted_iota(jnp.int32, (nrow, total_rows), 1) == source, 1.0, 0.0).astype(BF16)
     w3[...] = jnp.dot(pick, wl_v[...], preferred_element_type=F32).astype(BF16)
     w1t[...] = jnp.dot(pick, wf_v[...], preferred_element_type=F32).T.astype(BF16)
@@ -115,11 +115,11 @@
         base = pl.multiple_of(block * LANES, LANES)
         cols = pl.ds(base, LANES)
 
-        def group(g, carry):
-            rows = pl.ds(pl.multiple_of(16 * g, 16), 16)
+        for g in range(nrow // 16):
+            rows = slice(16 * g, 16 * g + 16)
             p = p16[rows, cols]
             tiles = [
-                ext[pl.ds(2 * g, 2), :, pl.ds(base + LANES * t, LANES)].reshape(16, LANES) for t in range(9)
+                ext[2 * g : 2 * g + 2, :, pl.ds(base + LANES * t, LANES)].reshape(16, LANES) for t in range(9)
             ]
             total = None
             for off, near, beyond in ((0, w00, w10), (1, w01, w11)):
@@ -134,9 +134,6 @@
                     term = weight[rows, cols] * value.astype(F32)
                     total = term if total is None else total + term
             adv[rows, cols] = total.astype(BF16)
-            return carry
-
-        lax.fori_loop(0, nrow // 16, group, 0)
         return cols
 
     def block_of(half, i):
@@ -272,8 +269,8 @@
     result = pl.pallas_call(
         functools.partial(kernel, nband, nlev),
         out_shape=jax.ShapeDtypeStruct((levels, nfield, ncols), BF16),
-        in_specs=[pl.BlockSpec(memory_space=pl.ANY)] * 8,
-        out_specs=pl.BlockSpec(memory_space=pl.ANY),
+        in_specs=[pl.BlockSpec(memory_space=pltpu.HBM)] * 8,
+        out_specs=pl.BlockSpec(memory_space=pltpu.HBM),
         scratch_shapes=[
             V((levels, nfield, 2 * ncols), BF16),
             V((levels, ncols), jnp.int32),
@@ -302,7 +299,7 @@
             DMA((2, 2)), DMA((2, 2)), DMA((2, 2)), DMA((2, 2)), DMA((2, 4)),
         ],
         compiler_params=pltpu.CompilerParams(
-            collective_id=0, has_side_effects=True, vmem_limit_bytes=40 << 20
+            collective_id=0, has_side_effects=True, vmem_limit_bytes=60 << 20
         ),
     )(
         fields.transpose(1, 0, 2),

time: 50.2 us -> 40 us (0.80)
  local copies, waits for them, and re-layouts: 7.38 us -> 1.89 us
  Pallas kernels: 42.5 us -> 38 us
    unnamed x17 -> x1, local copies, waits for them, and re-layouts: 7.38 us -> 1.89 us
    pallas_call x1, Pallas kernels: 42.5 us -> 38 us  [on_device(): pl.pallas_call(functools.partial(kernel, nband, nlev), out_shape=jax.Shap...]
where the time goes in v2:
time: 40 us; the launch traced here: 39.9 us
  Pallas kernels  38 us (95%)
  local copies, waits for them, and re-layouts  1.89 us (5%)
    pallas_call x1, Pallas kernels, on_device(): pl.pallas_call(functools.partial(kernel, nband, nlev), out_shape=jax.Shap...  38 us
    unnamed x1, local copies, waits for them, and re-layouts  1.89 us

profile of v2, /device:TPU:8, one launch (start us, length us, event | category | flops | bytes accessed | tf_op | source)
XLA Modules:
  0.0 39.9 jit_solution(8365690273758561480)
XLA Ops:
  0.0 38.0 %shard_map.82 = bf16[34,8,1024]{2,1,0:T(8,128)(2,1)} custom-call(bf16[34,8,1024]{2,1,0:T(8,128)(2,1)} %bitcast.8, s32[34,1024]{1,0:T(8,128)} %depart.1, bf16[34,2,1024]{2,1,0:T(2,128)(2,1)} %bitcast.11, bf16[1088,256]{1,0:T(8,128)(2,1)} %bitcast.9, bf16[1088,256]{1,0:T(8,128)(2,1)} %bitcast.10, bf16[256,256]{1,0:T(8,128)(2,1)} %w_middle.1, ...), custom_call_target="tpu_custom_call" | custom-call | tf_op jit(solution)/shard_map/pallas_call | solution.py:269
  38.0 1.9 %copy.10 = bf16[8,34,1024]{2,0,1:T(8,128)(2,1)} copy(bf16[8,34,1024]{2,0,1:T(8,128)(2,1)} %bitcast.7) | data formatting | bytes 1114112

commit v3 on v2

--- a/solution.py
+++ b/solution.py
@@ -34,9 +34,8 @@
 def kernel(
     nband, nlev, fields, depart, fraction, w_first, w_last, w_middle, b_first, b_middle, out,
     ext, dep_v, frac_v, wf_v, wl_v, wm_v, bf_v, bm_v, p16, w00, w01, w10, w11,
-    adv, w1t, w3, w2t, b1, b2, part, opp_tx, opp_rx, near_tx, near_rx, mid, out_v,
-    load_sem, halo_send, halo_recv, opp_send, opp_recv, near_send, near_recv,
-    mid_send, mid_recv, fwd_send, fwd_recv, store_sem,
+    adv, w1t, w3, w2t, b1, b2, part, part_tx, part_rx, mid, out_v,
+    load_sem, halo_send, halo_recv, part_send, part_recv, mid_send, mid_recv, store_sem,
 ):
     band, me = lax.axis_index("band"), lax.axis_index("lev")
     nrow = adv.shape[0]
@@ -46,21 +45,21 @@
     up, down, far = lax.rem(me + 1, nlev), lax.rem(me + nlev - 1, nlev), lax.rem(me + 2, nlev)
 
     barrier = pltpu.get_barrier_semaphore()
-    for peer in ({"band": east}, {"band": west}, {"lev": up}, {"lev": down}):
+    for peer in ({"band": east}, {"band": west}, {"lev": up}, {"lev": down}, {"lev": far}):
         pl.semaphore_signal(barrier, inc=1, device_id=peer, device_id_type=MESH)
 
     loads = [
         pltpu.make_async_copy(src, dst, load_sem.at[n])
         for n, (src, dst) in enumerate(
             (
-                (depart, dep_v), (fraction, frac_v), (w_first, wf_v), (w_last, wl_v), (w_middle, wm_v),
-                (b_first, bf_v), (b_middle, bm_v), (fields, ext.at[:, :, pl.ds(ROW, 2 * ROW)]),
+                (depart, dep_v), (fraction, frac_v), (fields, ext.at[:, :, pl.ds(ROW, 2 * ROW)]),
+                (w_first, wf_v), (w_last, wl_v), (w_middle, wm_v), (b_first, bf_v), (b_middle, bm_v),
             )
         )
     ]
     for load in loads:
         load.start()
-    pl.semaphore_wait(barrier, 4)
+    pl.semaphore_wait(barrier, 5)
 
     halos = []
     for i in range(4):
@@ -97,7 +96,7 @@
 
     lax.fori_loop(0, levels // 2, prepare, 0)
 
-    for load in loads[2:7]:
+    for load in loads[3:]:
         load.wait()
     total_rows = wf_v.shape[0]
     total_levels = total_rows // 8
@@ -109,7 +108,7 @@
     w2t[...] = wm_v[...].astype(F32).T.astype(BF16)
     b1[...] = jnp.broadcast_to(bf_v[...], (LANES, bf_v.shape[1])).T
     b2[...] = jnp.broadcast_to(bm_v[...], (LANES, bm_v.shape[1])).T
-    loads[7].wait()
+    loads[2].wait()
 
     def advect(block):
         base = pl.multiple_of(block * LANES, LANES)
@@ -159,60 +158,36 @@
             src_ref=src, dst_ref=dst, send_sem=send, recv_sem=recv, device_id={"lev": peer}, device_id_type=MESH
         )
 
-    hidden = w1t.shape[0]
-    top, bottom = pl.ds(0, hidden // 2), pl.ds(hidden // 2, hidden // 2)
-    sent = []
-
-    def send_far(half):
-        opp_tx[half] = part[half, far].astype(BF16)
-        for way, rows, peer in ((0, top, up), (1, bottom, down)):
-            copy = remote(
-                opp_tx.at[half, rows], opp_rx.at[half, way], opp_send.at[half, way], opp_recv.at[half, way], peer
-            )
-            copy.start()
-            sent.append(copy)
-
-    def send_near(half):
-        for way, rows, other, peer in ((0, top, bottom, up), (1, bottom, top, down)):
-            remote(
-                opp_tx.at[half, rows], opp_rx.at[half, way], opp_send.at[half, way], opp_recv.at[half, way], peer
-            ).wait_recv()
-            near_tx[half, way, rows] = (part[half, peer, rows] + opp_rx[half, way].astype(F32)).astype(BF16)
-            near_tx[half, way, other] = part[half, peer, other].astype(BF16)
-            copy = remote(
-                near_tx.at[half, way], near_rx.at[half, way], near_send.at[half, way], near_recv.at[half, way], peer
-            )
-            copy.start()
-            sent.append(copy)
+    def partial_copy(half, i):
+        slot = lax.rem(me - i + nlev, nlev)
+        return remote(
+            part_tx.at[half, i], part_rx.at[half, slot], part_send.at[half, i], part_recv.at[half, slot], i
+        )
+
+    def send_partial(half, i):
+        @pl.when(me != i)
+        def _():
+            part_tx[half, i] = part[half, i].astype(BF16)
+            partial_copy(half, i).start()
+
+    def middle_copy(half, owner, hop):
+        return remote(
+            mid.at[half, owner], mid.at[half, owner], mid_send.at[half, hop], mid_recv.at[half, owner],
+            lax.rem(owner + hop, nlev),
+        )
 
     def finish(half):
         total = part[half, me] + b1[...]
-        for way, peer in ((0, up), (1, down)):
+        for slot in range(1, nlev):
             remote(
-                near_tx.at[half, way], near_rx.at[half, way], near_send.at[half, way], near_recv.at[half, way], peer
+                part_tx.at[half, 0], part_rx.at[half, slot], part_send.at[half, 0], part_recv.at[half, slot], far
             ).wait_recv()
-            total = total + near_rx[half, way].astype(F32)
+            total = total + part_rx[half, slot].astype(F32)
         first = silu(total).astype(BF16)
         second = jnp.dot(w2t[...], first, preferred_element_type=F32) + b2[...]
         mid[half, me] = silu(second).astype(BF16)
-        for way, peer in ((0, up), (1, down)):
-            copy = remote(
-                mid.at[half, me], mid.at[half, me], mid_send.at[half, way], mid_recv.at[half, way], peer
-            )
-            copy.start()
-            sent.append(copy)
-
-    def pass_on(half):
-        for way, rows, owner, peer in ((0, top, down, up), (1, bottom, up, down)):
-            remote(
-                mid.at[half, owner], mid.at[half, owner], mid_send.at[half, way], mid_recv.at[half, way], peer
-            ).wait_recv()
-            copy = remote(
-                mid.at[half, owner, rows], mid.at[half, owner, rows],
-                fwd_send.at[half, way], fwd_recv.at[half, way], peer,
-            )
-            copy.start()
-            sent.append(copy)
+        for hop in (2, 1, 3):
+            middle_copy(half, me, hop).start()
 
     stores = []
 
@@ -228,33 +203,28 @@
 
     def finale(half):
         last(half, me)
-        last(half, up)
-        last(half, down)
-        for way, rows, peer in ((0, top, up), (1, bottom, down)):
-            remote(
-                mid.at[half, far, rows], mid.at[half, far, rows],
-                fwd_send.at[half, way], fwd_recv.at[half, way], peer,
-            ).wait_recv()
-        last(half, far)
-
-    for i in range(4):
-        forward(0, i)
-    send_far(0)
-    forward(1, 0)
-    send_near(0)
-    forward(1, 1)
-    forward(1, 2)
+        for hop in (1, 3, 2):
+            owner = lax.rem(me + hop, nlev)
+            middle_copy(half, owner, nlev - hop).wait_recv()
+            last(half, owner)
+
+    for half in range(2):
+        for i in range(nlev):
+            forward(half, i)
+            send_partial(half, i)
     finish(0)
-    forward(1, 3)
-    send_far(1)
-    pass_on(0)
-    send_near(1)
+    finish(1)
     finale(0)
-    finish(1)
-    pass_on(1)
     finale(1)
 
-    for copy in halos + sent:
+    for half in range(2):
+        for i in range(nlev):
+            @pl.when(me != i)
+            def _():
+                partial_copy(half, i).wait_send()
+        for hop in range(1, nlev):
+            middle_copy(half, me, hop).wait_send()
+    for copy in halos:
         copy.wait_send()
     for store in stores:
         store.wait()
@@ -289,14 +259,11 @@
             V((hidden, LANES), F32),
             V((hidden, LANES), F32),
             V((2, 4, hidden, LANES), F32),
-            V((2, hidden, LANES), BF16),
-            V((2, 2, hidden // 2, LANES), BF16),
-            V((2, 2, hidden, LANES), BF16),
-            V((2, 2, hidden, LANES), BF16),
+            V((2, 4, hidden, LANES), BF16),
+            V((2, 4, hidden, LANES), BF16),
             V((2, 4, hidden, LANES), BF16),
             V((levels, nfield, ncols), BF16),
-            DMA((8,)), DMA((2, 4)), DMA((2, 4)), DMA((2, 2)), DMA((2, 2)), DMA((2, 2)), DMA((2, 2)),
-            DMA((2, 2)), DMA((2, 2)), DMA((2, 2)), DMA((2, 2)), DMA((2, 4)),
+            DMA((8,)), DMA((2, 4)), DMA((2, 4)), DMA((2, 4)), DMA((2, 4)), DMA((2, 4)), DMA((2, 4)), DMA((2, 4)),
         ],
         compiler_params=pltpu.CompilerParams(
             collective_id=0, has_side_effects=True, vmem_limit_bytes=60 << 20

time: 40 us -> 30 us (0.75)
  Pallas kernels: 38 us -> 27.9 us
    pallas_call x1, Pallas kernels: 38 us -> 27.9 us  [on_device(): pl.pallas_call(functools.partial(kernel, nband, nlev), out_shape=jax.Shap...]
where the time goes in v3:
time: 30 us; the launch traced here: 29.8 us
  Pallas kernels  27.9 us (93%)
  local copies, waits for them, and re-layouts  1.89 us (6%)
    pallas_call x1, Pallas kernels, on_device(): pl.pallas_call(functools.partial(kernel, nband, nlev), out_shape=jax.Shap...  27.9 us
    unnamed x1, local copies, waits for them, and re-layouts  1.89 us

profile of v3, /device:TPU:8, one launch (start us, length us, event | category | flops | bytes accessed | tf_op | source)
XLA Modules:
  0.0 29.8 jit_solution(4060719355806279161)
XLA Ops:
  0.0 27.9 %shard_map.82 = bf16[34,8,1024]{2,1,0:T(8,128)(2,1)} custom-call(bf16[34,8,1024]{2,1,0:T(8,128)(2,1)} %bitcast.8, s32[34,1024]{1,0:T(8,128)} %depart.1, bf16[34,2,1024]{2,1,0:T(2,128)(2,1)} %bitcast.11, bf16[1088,256]{1,0:T(8,128)(2,1)} %bitcast.9, bf16[1088,256]{1,0:T(8,128)(2,1)} %bitcast.10, bf16[256,256]{1,0:T(8,128)(2,1)} %w_middle.1, ...), custom_call_target="tpu_custom_call" | custom-call | tf_op jit(solution)/shard_map/pallas_call | solution.py:239
  27.9 1.9 %copy.10 = bf16[8,34,1024]{2,0,1:T(8,128)(2,1)} copy(bf16[8,34,1024]{2,0,1:T(8,128)(2,1)} %bitcast.7) | data formatting | bytes 1114112

commit v4 on v3

--- a/solution.py
+++ b/solution.py
@@ -10,6 +10,7 @@
 MESH = pl.DeviceIdType.MESH
 F32, BF16 = jnp.float32, jnp.bfloat16
 LANES = 128
+WINDOW = 48
 ROW = 512
 
 _PICK = lax.GatherDimensionNumbers(
@@ -34,8 +35,9 @@
 def kernel(
     nband, nlev, fields, depart, fraction, w_first, w_last, w_middle, b_first, b_middle, out,
     ext, dep_v, frac_v, wf_v, wl_v, wm_v, bf_v, bm_v, p16, w00, w01, w10, w11,
-    adv, w1t, w3, w2t, b1, b2, part, part_tx, part_rx, mid, out_v,
-    load_sem, halo_send, halo_recv, part_send, part_recv, mid_send, mid_recv, store_sem,
+    adv, w1t, w3, w2t, b1, b2, part, part_tx, part_rx, mid,
+    load_sem, halo_send, halo_recv, part_send, part_recv, mid_send, mid_recv,
+    west_in, peers_in, lev_in,
 ):
     band, me = lax.axis_index("band"), lax.axis_index("lev")
     nrow = adv.shape[0]
@@ -44,39 +46,59 @@
     east, west = lax.rem(band + 1, nband), lax.rem(band + nband - 1, nband)
     up, down, far = lax.rem(me + 1, nlev), lax.rem(me + nlev - 1, nlev), lax.rem(me + 2, nlev)
 
+    is_first = core == 0
     barrier = pltpu.get_barrier_semaphore()
-    for peer in ({"band": east}, {"band": west}, {"lev": up}, {"lev": down}, {"lev": far}):
-        pl.semaphore_signal(barrier, inc=1, device_id=peer, device_id_type=MESH)
-
+    others = [lax.rem(me + hop, nlev) for hop in range(1, nlev)]
+
+    def tell(sem, peer):
+        pl.semaphore_signal(sem, inc=1, device_id=peer, device_id_type=MESH)
+
+    @pl.when(is_first)
+    def _():
+        tell(barrier, {"band": west})
+        tell(barrier, {"band": east})
+        for peer in others:
+            tell(barrier, {"lev": peer})
+
+    @pl.when(jnp.logical_not(is_first))
+    def _():
+        tell(barrier, {"band": west})
+
+    pairs_of_refs = [(depart, dep_v), (fraction, frac_v), (fields, ext.at[:, :, pl.ds(ROW, 2 * ROW)])]
+    for src, dst in ((w_first, wf_v), (w_last, wl_v)):
+        for f in range(8):
+            start = pl.multiple_of((f * nlev * levels + me * levels) // 16 * 16, 16)
+            pairs_of_refs.append((src.at[pl.ds(start, WINDOW)], dst.at[pl.ds(f * WINDOW, WINDOW)]))
+    pairs_of_refs += [(w_middle, wm_v), (b_first, bf_v), (b_middle, bm_v)]
     loads = [
-        pltpu.make_async_copy(src, dst, load_sem.at[n])
-        for n, (src, dst) in enumerate(
-            (
-                (depart, dep_v), (fraction, frac_v), (fields, ext.at[:, :, pl.ds(ROW, 2 * ROW)]),
-                (w_first, wf_v), (w_last, wl_v), (w_middle, wm_v), (b_first, bf_v), (b_middle, bm_v),
-            )
-        )
+        pltpu.make_async_copy(src, dst, load_sem.at[n]) for n, (src, dst) in enumerate(pairs_of_refs)
     ]
     for load in loads:
         load.start()
-    pl.semaphore_wait(barrier, 5)
-
-    halos = []
-    for i in range(4):
-        for side, peer, src, dst in ((0, east, 7 - i, 3 - i), (1, west, i, 12 + i)):
-            copy = pltpu.make_async_remote_copy(
-                src_ref=fields.at[:, :, pl.ds(src * LANES, LANES)],
-                dst_ref=ext.at[:, :, pl.ds(dst * LANES, LANES)],
-                send_sem=halo_send.at[side, i],
-                recv_sem=halo_recv.at[side, i],
-                device_id={"band": peer},
-                device_id_type=MESH,
-            )
-            copy.start()
-            halos.append(copy)
-
-    loads[0].wait()
-    loads[1].wait()
+
+    @pl.when(is_first)
+    def _():
+        pl.semaphore_wait(barrier, nlev)
+        for peer in others:
+            tell(peers_in, {"lev": peer})
+
+    @pl.when(jnp.logical_not(is_first))
+    def _():
+        pl.semaphore_wait(barrier, 2)
+        tell(west_in, {"band": east})
+
+
+    def halo_copy(right, i, tiles=1):
+        src = right * (8 - tiles - i) + (1 - right) * i
+        dst = right * (4 - tiles - i) + (1 - right) * (12 + i)
+        return pltpu.make_async_remote_copy(
+            src_ref=fields.at[:, :, pl.ds(pl.multiple_of(src * LANES, LANES), tiles * LANES)],
+            dst_ref=ext.at[:, :, pl.ds(pl.multiple_of(dst * LANES, LANES), tiles * LANES)],
+            send_sem=halo_send.at[tiles // 4, i],
+            recv_sem=halo_recv.at[tiles // 4, i],
+            device_id={"band": right * east + (1 - right) * west},
+            device_id_type=MESH,
+        )
 
     def prepare(i, carry):
         lane = lax.rem(lax.broadcasted_iota(jnp.int32, (8, 2 * ROW), 1), LANES) + ROW
@@ -94,17 +116,29 @@
             ref[rows, :] = jnp.concatenate([one, two], axis=0)
         return carry
 
+    def send_slow():
+        @pl.when(is_first)
+        def _():
+            pl.semaphore_wait(west_in, 1)
+
+        for i in range(4):
+            halo_copy(core, i).start()
+
+    ahead = lax.rem(band, 16) == 0
+    halo_copy(1 - core, 0, 4).start()
+    pl.when(jnp.logical_not(ahead))(send_slow)
+    loads[0].wait()
+    loads[1].wait()
     lax.fori_loop(0, levels // 2, prepare, 0)
 
     for load in loads[3:]:
         load.wait()
-    total_rows = wf_v.shape[0]
-    total_levels = total_rows // 8
-    r = lax.broadcasted_iota(jnp.int32, (nrow, total_rows), 0)
-    source = (r & 7) * total_levels + me * levels + (r >> 3)
-    pick = jnp.where(lax.broadcasted_iota(jnp.int32, (nrow, total_rows), 1) == source, 1.0, 0.0).astype(BF16)
+    r = lax.broadcasted_iota(jnp.int32, (nrow, 8 * WINDOW), 0)
+    field = r & 7
+    source = field * WINDOW + (field & 1) * 8 + me * 2 + (r >> 3)
+    pick = jnp.where(lax.broadcasted_iota(jnp.int32, (nrow, 8 * WINDOW), 1) == source, 1.0, 0.0).astype(BF16)
+    w1t[...] = jnp.dot(pick, wf_v[...], preferred_element_type=F32).T.astype(BF16)
     w3[...] = jnp.dot(pick, wl_v[...], preferred_element_type=F32).astype(BF16)
-    w1t[...] = jnp.dot(pick, wf_v[...], preferred_element_type=F32).T.astype(BF16)
     w2t[...] = wm_v[...].astype(F32).T.astype(BF16)
     b1[...] = jnp.broadcast_to(bf_v[...], (LANES, bf_v.shape[1])).T
     b2[...] = jnp.broadcast_to(bm_v[...], (LANES, bm_v.shape[1])).T
@@ -141,15 +175,10 @@
 
     def forward(half, i):
         right, block = block_of(half, i)
-        tile = right * (12 + i) + (1 - right) * (3 - i)
-        pltpu.make_async_remote_copy(
-            src_ref=fields.at[:, :, pl.ds(0, LANES)],
-            dst_ref=ext.at[:, :, pl.ds(pl.multiple_of(tile * LANES, LANES), LANES)],
-            send_sem=halo_send.at[right, i],
-            recv_sem=halo_recv.at[right, i],
-            device_id={"band": east},
-            device_id_type=MESH,
-        ).wait_recv()
+        if half == 1:
+            halo_copy(1 - right, i).wait_recv()
+        elif i == 0:
+            halo_copy(1 - right, 0, 4).wait_recv()
         cols = advect(block)
         part[half, i] = jnp.dot(w1t[...], adv[:, cols], preferred_element_type=F32)
 
@@ -189,17 +218,12 @@
         for hop in (2, 1, 3):
             middle_copy(half, me, hop).start()
 
-    stores = []
-
     def last(half, i):
         _, block = block_of(half, i)
         cols = pl.ds(pl.multiple_of(block * LANES, LANES), LANES)
         tendency = jnp.dot(w3[...], mid[half, i], preferred_element_type=F32)
         updated = (adv[:, cols].astype(F32) + tendency).astype(BF16)
-        out_v[:, :, cols] = updated.reshape(levels, 8, LANES)
-        store = pltpu.make_async_copy(out_v.at[:, :, cols], out.at[:, :, cols], store_sem.at[half, i])
-        store.start()
-        stores.append(store)
+        out[:, :, cols] = updated.reshape(levels, 8, LANES)
 
     def finale(half):
         last(half, me)
@@ -208,10 +232,23 @@
             middle_copy(half, owner, nlev - hop).wait_recv()
             last(half, owner)
 
-    for half in range(2):
-        for i in range(nlev):
-            forward(half, i)
-            send_partial(half, i)
+    @pl.when(is_first)
+    def _():
+        pl.semaphore_wait(peers_in, nlev - 1)
+        tell(lev_in, {"band": east})
+
+    for i in range(nlev):
+        forward(0, i)
+        if i == 0:
+            @pl.when(jnp.logical_not(is_first))
+            def _():
+                pl.semaphore_wait(lev_in, 1)
+
+        send_partial(0, i)
+    pl.when(ahead)(send_slow)
+    for i in range(nlev):
+        forward(1, i)
+        send_partial(1, i)
     finish(0)
     finish(1)
     finale(0)
@@ -224,10 +261,9 @@
                 partial_copy(half, i).wait_send()
         for hop in range(1, nlev):
             middle_copy(half, me, hop).wait_send()
-    for copy in halos:
-        copy.wait_send()
-    for store in stores:
-        store.wait()
+    halo_copy(1 - core, 0, 4).wait_send()
+    for i in range(4):
+        halo_copy(core, i).wait_send()
 
 
 def on_device(nband, nlev, fields, depart, fraction, w_first, b_first, w_middle, b_middle, w_last):
@@ -235,18 +271,28 @@
     nrow, hidden = nfield * levels, w_middle.shape[0]
     V, DMA = pltpu.VMEM, pltpu.SemaphoreType.DMA
     table = V((nrow, ncols), F32)
-    whole = V((nfield * w_first.shape[1], hidden), BF16)
+    window = V((nfield * WINDOW, hidden), BF16)
+    operands = (
+        fields.transpose(1, 0, 2),
+        depart,
+        fraction.transpose(1, 0, 2),
+        w_first.reshape(-1, hidden),
+        w_last.reshape(-1, hidden),
+        w_middle,
+        b_first[None, :],
+        b_middle[None, :],
+    )
     result = pl.pallas_call(
         functools.partial(kernel, nband, nlev),
         out_shape=jax.ShapeDtypeStruct((levels, nfield, ncols), BF16),
         in_specs=[pl.BlockSpec(memory_space=pltpu.HBM)] * 8,
-        out_specs=pl.BlockSpec(memory_space=pltpu.HBM),
+        out_specs=pl.BlockSpec(memory_space=pltpu.VMEM),
         scratch_shapes=[
             V((levels, nfield, 2 * ncols), BF16),
             V((levels, ncols), jnp.int32),
             V((levels, 2, ncols), BF16),
-            whole,
-            whole,
+            window,
+            window,
             V((hidden, hidden), BF16),
             V((1, hidden), F32),
             V((1, hidden), F32),
@@ -262,21 +308,14 @@
             V((2, 4, hidden, LANES), BF16),
             V((2, 4, hidden, LANES), BF16),
             V((2, 4, hidden, LANES), BF16),
-            V((levels, nfield, ncols), BF16),
-            DMA((8,)), DMA((2, 4)), DMA((2, 4)), DMA((2, 4)), DMA((2, 4)), DMA((2, 4)), DMA((2, 4)), DMA((2, 4)),
+            DMA((22,)), DMA((2, 4)), DMA((2, 4)), DMA((2, 4)), DMA((2, 4)), DMA((2, 4)), DMA((2, 4)),
+            pltpu.SemaphoreType.REGULAR, pltpu.SemaphoreType.REGULAR, pltpu.SemaphoreType.REGULAR,
         ],
         compiler_params=pltpu.CompilerParams(
-            collective_id=0, has_side_effects=True, vmem_limit_bytes=60 << 20
+            collective_id=0, has_side_effects=True, vmem_limit_bytes=40 << 20
         ),
     )(
-        fields.transpose(1, 0, 2),
-        depart,
-        fraction.transpose(1, 0, 2),
-        w_first.reshape(-1, hidden),
-        w_last.reshape(-1, hidden),
-        w_middle,
-        b_first[None, :],
-        b_middle[None, :],
+        *(pltpu.with_memory_space_constraint(x, pltpu.HBM) for x in operands)
     )
     return result.transpose(1, 0, 2)
 

time: 30 us -> 25.2 us (0.84)
  Pallas kernels: 27.9 us -> 24.1 us
  local copies, waits for them, and re-layouts: 1.89 us -> 0.81 us
    pallas_call x1, Pallas kernels: 27.9 us -> 24.1 us  [on_device(): pl.pallas_call(functools.partial(kernel, nband, nlev), out_shape=jax.Shap...]
    unnamed x1, local copies, waits for them, and re-layouts: 1.89 us -> 0.81 us
where the time goes in v4:
time: 25.2 us; the launch traced here: 24.9 us
  Pallas kernels  24.1 us (96%)
  local copies, waits for them, and re-layouts  0.81 us (3%)
    pallas_call x1, Pallas kernels, on_device(): pl.pallas_call(functools.partial(kernel, nband, nlev), out_shape=jax.Shap...  24.1 us
    unnamed x1, local copies, waits for them, and re-layouts  0.81 us

profile of v4, /device:TPU:8, one launch (start us, length us, event | category | flops | bytes accessed | tf_op | source)
XLA Modules:
  0.0 24.9 jit_solution(3697775942076888741)
XLA Ops:
  0.0 24.1 %shard_map.82 = bf16[34,8,1024]{2,1,0:T(8,128)(2,1)S(1)} custom-call(bf16[34,8,1024]{2,1,0:T(8,128)(2,1)} %bitcast.8, s32[34,1024]{1,0:T(8,128)} %depart.1, bf16[34,2,1024]{2,1,0:T(2,128)(2,1)} %bitcast.11, bf16[1088,256]{1,0:T(8,128)(2,1)} %bitcast.9, bf16[1088,256]{1,0:T(8,128)(2,1)} %bitcast.10, bf16[256,256]{1,0:T(8,128)(2,1)} %w_middle.1, ...), custom_call_target="tpu_custom_call" | custom-call | tf_op jit(solution)/shard_map/pallas_call | solution.py:285
  24.1 0.8 %copy.10 = bf16[8,34,1024]{2,0,1:T(8,128)(2,1)} copy(bf16[8,34,1024]{2,0,1:T(8,128)(2,1)S(1)} %bitcast.7) | data formatting | bytes 1114112

commit v5 on v4

--- a/solution.py
+++ b/solution.py
@@ -11,6 +11,7 @@
 F32, BF16 = jnp.float32, jnp.bfloat16
 LANES = 128
 WINDOW = 48
+QUARTER = 64
 ROW = 512
 
 _PICK = lax.GatherDimensionNumbers(
@@ -35,7 +36,7 @@
 def kernel(
     nband, nlev, fields, depart, fraction, w_first, w_last, w_middle, b_first, b_middle, out,
     ext, dep_v, frac_v, wf_v, wl_v, wm_v, bf_v, bm_v, p16, w00, w01, w10, w11,
-    adv, w1t, w3, w2t, b1, b2, part, part_tx, part_rx, mid,
+    adv, w1, w3, part, part_tx, part_rx, mid,
     load_sem, halo_send, halo_recv, part_send, part_recv, mid_send, mid_recv,
     west_in, peers_in, lev_in,
 ):
@@ -44,7 +45,6 @@
     levels = nrow // 8
     core = lax.rem(band, 2)
     east, west = lax.rem(band + 1, nband), lax.rem(band + nband - 1, nband)
-    up, down, far = lax.rem(me + 1, nlev), lax.rem(me + nlev - 1, nlev), lax.rem(me + 2, nlev)
 
     is_first = core == 0
     barrier = pltpu.get_barrier_semaphore()
@@ -137,11 +137,8 @@
     field = r & 7
     source = field * WINDOW + (field & 1) * 8 + me * 2 + (r >> 3)
     pick = jnp.where(lax.broadcasted_iota(jnp.int32, (nrow, 8 * WINDOW), 1) == source, 1.0, 0.0).astype(BF16)
-    w1t[...] = jnp.dot(pick, wf_v[...], preferred_element_type=F32).T.astype(BF16)
+    w1[...] = jnp.dot(pick, wf_v[...], preferred_element_type=F32).astype(BF16)
     w3[...] = jnp.dot(pick, wl_v[...], preferred_element_type=F32).astype(BF16)
-    w2t[...] = wm_v[...].astype(F32).T.astype(BF16)
-    b1[...] = jnp.broadcast_to(bf_v[...], (LANES, bf_v.shape[1])).T
-    b2[...] = jnp.broadcast_to(bm_v[...], (LANES, bm_v.shape[1])).T
     loads[2].wait()
 
     def advect(block):
@@ -167,100 +164,99 @@
                     term = weight[rows, cols] * value.astype(F32)
                     total = term if total is None else total + term
             adv[rows, cols] = total.astype(BF16)
-        return cols
-
-    def block_of(half, i):
-        right = (1 - core) if half == 0 else core
-        return right, right * (4 + i) + (1 - right) * (3 - i)
-
-    def forward(half, i):
-        right, block = block_of(half, i)
-        if half == 1:
-            halo_copy(1 - right, i).wait_recv()
-        elif i == 0:
-            halo_copy(1 - right, 0, 4).wait_recv()
-        cols = advect(block)
-        part[half, i] = jnp.dot(w1t[...], adv[:, cols], preferred_element_type=F32)
+
+    def columns(unit):
+        right = (1 - core) if unit < 2 else core
+        k = unit % 2
+        block = right * (4 + 2 * k) + (1 - right) * (2 - 2 * k)
+        return pl.ds(pl.multiple_of(block * LANES, 2 * LANES), 2 * LANES)
 
     def remote(src, dst, send, recv, peer):
         return pltpu.make_async_remote_copy(
             src_ref=src, dst_ref=dst, send_sem=send, recv_sem=recv, device_id={"lev": peer}, device_id_type=MESH
         )
 
-    def partial_copy(half, i):
-        slot = lax.rem(me - i + nlev, nlev)
+    def partial_copy(unit, hop):
         return remote(
-            part_tx.at[half, i], part_rx.at[half, slot], part_send.at[half, i], part_recv.at[half, slot], i
-        )
-
-    def send_partial(half, i):
-        @pl.when(me != i)
-        def _():
-            part_tx[half, i] = part[half, i].astype(BF16)
-            partial_copy(half, i).start()
-
-    def middle_copy(half, owner, hop):
+            part_tx.at[unit, hop], part_rx.at[unit, nlev - hop],
+            part_send.at[unit, hop], part_recv.at[unit, nlev - hop], lax.rem(me + hop, nlev),
+        )
+
+    def middle_copy(unit, owner, hop):
         return remote(
-            mid.at[half, owner], mid.at[half, owner], mid_send.at[half, hop], mid_recv.at[half, owner],
+            mid.at[unit, owner], mid.at[unit, owner], mid_send.at[unit, hop], mid_recv.at[unit, owner],
             lax.rem(owner + hop, nlev),
         )
 
-    def finish(half):
-        total = part[half, me] + b1[...]
-        for slot in range(1, nlev):
-            remote(
-                part_tx.at[half, 0], part_rx.at[half, slot], part_send.at[half, 0], part_recv.at[half, slot], far
-            ).wait_recv()
-            total = total + part_rx[half, slot].astype(F32)
+    def quarter(peer):
+        return pl.ds(pl.multiple_of(peer * QUARTER, QUARTER), QUARTER)
+
+    def forward(unit):
+        right = (1 - core) if unit < 2 else core
+        for i in (2 * (unit % 2), 2 * (unit % 2) + 1):
+            if unit >= 2:
+                halo_copy(1 - right, i).wait_recv()
+            elif i == 0:
+                halo_copy(1 - right, 0, 4).wait_recv()
+            advect(right * (4 + i) + (1 - right) * (3 - i))
+        part[unit] = lax.dot_general(
+            adv[:, columns(unit)], w1[...], (((0,), (0,)), ((), ())), preferred_element_type=F32
+        )
+
+    def send_partial(unit):
+        for hop in (2, 1, 3):
+            part_tx[unit, hop] = part[unit, quarter(lax.rem(me + hop, nlev)), :].astype(BF16)
+            partial_copy(unit, hop).start()
+
+    def complete(unit):
+        total = part[unit, quarter(me), :] + bf_v[...]
+        for hop in (1, 3, 2):
+            partial_copy(unit, hop).wait_recv()
+            total = total + part_rx[unit, nlev - hop].astype(F32)
         first = silu(total).astype(BF16)
-        second = jnp.dot(w2t[...], first, preferred_element_type=F32) + b2[...]
-        mid[half, me] = silu(second).astype(BF16)
+        second = jnp.dot(first, wm_v[...], preferred_element_type=F32) + bm_v[...]
+        mid[unit, me] = silu(second).astype(BF16)
         for hop in (2, 1, 3):
-            middle_copy(half, me, hop).start()
-
-    def last(half, i):
-        _, block = block_of(half, i)
-        cols = pl.ds(pl.multiple_of(block * LANES, LANES), LANES)
-        tendency = jnp.dot(w3[...], mid[half, i], preferred_element_type=F32)
+            middle_copy(unit, me, hop).start()
+
+    def last(unit):
+        for hop in (1, 3, 2):
+            middle_copy(unit, lax.rem(me + hop, nlev), nlev - hop).wait_recv()
+        cols = columns(unit)
+        tendency = lax.dot_general(
+            w3[...], mid[unit].reshape(2 * LANES, w3.shape[1]), (((1,), (1,)), ((), ())), preferred_element_type=F32
+        )
         updated = (adv[:, cols].astype(F32) + tendency).astype(BF16)
-        out[:, :, cols] = updated.reshape(levels, 8, LANES)
-
-    def finale(half):
-        last(half, me)
-        for hop in (1, 3, 2):
-            owner = lax.rem(me + hop, nlev)
-            middle_copy(half, owner, nlev - hop).wait_recv()
-            last(half, owner)
+        out[:, :, cols] = updated.reshape(levels, 8, 2 * LANES)
+
+    forward(0)
 
     @pl.when(is_first)
     def _():
         pl.semaphore_wait(peers_in, nlev - 1)
         tell(lev_in, {"band": east})
 
-    for i in range(nlev):
-        forward(0, i)
-        if i == 0:
-            @pl.when(jnp.logical_not(is_first))
-            def _():
-                pl.semaphore_wait(lev_in, 1)
-
-        send_partial(0, i)
+    @pl.when(jnp.logical_not(is_first))
+    def _():
+        pl.semaphore_wait(lev_in, 1)
+
+    send_partial(0)
+    forward(1)
+    send_partial(1)
     pl.when(ahead)(send_slow)
-    for i in range(nlev):
-        forward(1, i)
-        send_partial(1, i)
-    finish(0)
-    finish(1)
-    finale(0)
-    finale(1)
-
-    for half in range(2):
-        for i in range(nlev):
-            @pl.when(me != i)
-            def _():
-                partial_copy(half, i).wait_send()
+    forward(2)
+    send_partial(2)
+    forward(3)
+    send_partial(3)
+    for unit in range(4):
+        complete(unit)
+    for unit in range(4):
+        last(unit)
+
+    for unit in range(4):
         for hop in range(1, nlev):
-            middle_copy(half, me, hop).wait_send()
+            partial_copy(unit, hop).wait_send()
+            middle_copy(unit, me, hop).wait_send()
     halo_copy(1 - core, 0, 4).wait_send()
     for i in range(4):
         halo_copy(core, i).wait_send()
@@ -299,16 +295,13 @@
             V((nrow, ncols), jnp.int16),
             table, table, table, table,
             V((nrow, ncols), BF16),
-            V((hidden, nrow), BF16),
             V((nrow, hidden), BF16),
-            V((hidden, hidden), BF16),
-            V((hidden, LANES), F32),
-            V((hidden, LANES), F32),
-            V((2, 4, hidden, LANES), F32),
-            V((2, 4, hidden, LANES), BF16),
-            V((2, 4, hidden, LANES), BF16),
-            V((2, 4, hidden, LANES), BF16),
-            DMA((22,)), DMA((2, 4)), DMA((2, 4)), DMA((2, 4)), DMA((2, 4)), DMA((2, 4)), DMA((2, 4)),
+            V((nrow, hidden), BF16),
+            V((4, 2 * LANES, hidden), F32),
+            V((4, 4, QUARTER, hidden), BF16),
+            V((4, 4, QUARTER, hidden), BF16),
+            V((4, 4, QUARTER, hidden), BF16),
+            DMA((22,)), DMA((2, 4)), DMA((2, 4)), DMA((4, 4)), DMA((4, 4)), DMA((4, 4)), DMA((4, 4)),
             pltpu.SemaphoreType.REGULAR, pltpu.SemaphoreType.REGULAR, pltpu.SemaphoreType.REGULAR,
         ],
         compiler_params=pltpu.CompilerParams(

time: 25.2 us -> 24 us (0.952)
  Pallas kernels: 24.1 us -> 22.9 us
    pallas_call x1, Pallas kernels: 24.1 us -> 22.9 us  [on_device(): pl.pallas_call(functools.partial(kernel, nband, nlev), out_shape=jax.Shap...]
where the time goes in v5:
time: 24 us; the launch traced here: 23.8 us
  Pallas kernels  22.9 us (95%)
  local copies, waits for them, and re-layouts  0.81 us (3%)
    pallas_call x1, Pallas kernels, on_device(): pl.pallas_call(functools.partial(kernel, nband, nlev), out_shape=jax.Shap...  22.9 us
    unnamed x1, local copies, waits for them, and re-layouts  0.81 us

profile of v5, /device:TPU:8, one launch (start us, length us, event | category | flops | bytes accessed | tf_op | source)
XLA Modules:
  0.0 23.8 jit_solution(15020438132527215885)
XLA Ops:
  0.0 22.9 %shard_map.82 = bf16[34,8,1024]{2,1,0:T(8,128)(2,1)S(1)} custom-call(bf16[34,8,1024]{2,1,0:T(8,128)(2,1)} %bitcast.8, s32[34,1024]{1,0:T(8,128)} %depart.1, bf16[34,2,1024]{2,1,0:T(2,128)(2,1)} %bitcast.11, bf16[1088,256]{1,0:T(8,128)(2,1)} %bitcast.9, bf16[1088,256]{1,0:T(8,128)(2,1)} %bitcast.10, bf16[256,256]{1,0:T(8,128)(2,1)} %w_middle.1, ...), custom_call_target="tpu_custom_call" | custom-call | tf_op jit(solution)/shard_map/pallas_call | solution.py:281
  22.9 0.8 %copy.10 = bf16[8,34,1024]{2,0,1:T(8,128)(2,1)} copy(bf16[8,34,1024]{2,0,1:T(8,128)(2,1)S(1)} %bitcast.7) | data formatting | bytes 1114112

commit v6 on v5

--- a/solution.py
+++ b/solution.py
@@ -11,7 +11,10 @@
 F32, BF16 = jnp.float32, jnp.bfloat16
 LANES = 128
 WINDOW = 48
-QUARTER = 64
+QUARTER = 32
+BLOCKS = (2, 2, 2, 1, 1)
+HALF = 2
+STARTS = (0, 64, 128, 192, 224)
 ROW = 512
 
 _PICK = lax.GatherDimensionNumbers(
@@ -60,9 +63,17 @@
         for peer in others:
             tell(barrier, {"lev": peer})
 
+    place = lax.rem(band, 16)
+    ahead, late = place == 0, place == 15
+    greets_east, greeted = jnp.logical_and(core == 1, place != 15), jnp.logical_and(is_first, place != 0)
+
     @pl.when(jnp.logical_not(is_first))
     def _():
         tell(barrier, {"band": west})
+
+    @pl.when(greets_east)
+    def _():
+        tell(barrier, {"band": east})
 
     pairs_of_refs = [(depart, dep_v), (fraction, frac_v), (fields, ext.at[:, :, pl.ds(ROW, 2 * ROW)])]
     for src, dst in ((w_first, wf_v), (w_last, wl_v)):
@@ -73,21 +84,6 @@
     loads = [
         pltpu.make_async_copy(src, dst, load_sem.at[n]) for n, (src, dst) in enumerate(pairs_of_refs)
     ]
-    for load in loads:
-        load.start()
-
-    @pl.when(is_first)
-    def _():
-        pl.semaphore_wait(barrier, nlev)
-        for peer in others:
-            tell(peers_in, {"lev": peer})
-
-    @pl.when(jnp.logical_not(is_first))
-    def _():
-        pl.semaphore_wait(barrier, 2)
-        tell(west_in, {"band": east})
-
-
     def halo_copy(right, i, tiles=1):
         src = right * (8 - tiles - i) + (1 - right) * i
         dst = right * (4 - tiles - i) + (1 - right) * (12 + i)
@@ -117,16 +113,47 @@
         return carry
 
     def send_slow():
-        @pl.when(is_first)
+        for i, tiles in ((0, 2), (2, 1), (3, 1)):
+            halo_copy(core, i, tiles).start()
+
+    def answer_west():
+        pl.semaphore_wait(west_in, 1)
+        send_slow()
+
+    def start_loads():
+        for load in loads:
+            load.start()
+
+    pl.when(jnp.logical_not(late))(start_loads)
+
+    @pl.when(jnp.logical_not(is_first))
+    def _():
+        pl.semaphore_wait(barrier, 2)
+
+        @pl.when(jnp.logical_not(greets_east))
         def _():
-            pl.semaphore_wait(west_in, 1)
-
-        for i in range(4):
-            halo_copy(core, i).start()
-
-    ahead = lax.rem(band, 16) == 0
-    halo_copy(1 - core, 0, 4).start()
-    pl.when(jnp.logical_not(ahead))(send_slow)
+            tell(west_in, {"band": east})
+
+        send_slow()
+        halo_copy(1 - core, 0, 4).start()
+
+    pl.when(late)(start_loads)
+
+    @pl.when(is_first)
+    def _():
+        @pl.when(greeted)
+        def _():
+            pl.semaphore_wait(barrier, nlev + 1)
+            send_slow()
+
+        @pl.when(ahead)
+        def _():
+            pl.semaphore_wait(barrier, nlev)
+
+        for peer in others:
+            tell(peers_in, {"lev": peer})
+        halo_copy(1 - core, 0, 4).start()
+
     loads[0].wait()
     loads[1].wait()
     lax.fori_loop(0, levels // 2, prepare, 0)
@@ -142,14 +169,14 @@
     loads[2].wait()
 
     def advect(block):
-        base = pl.multiple_of(block * LANES, LANES)
-        cols = pl.ds(base, LANES)
+        base = block * LANES
+        cols = slice(base, base + LANES)
 
         for g in range(nrow // 16):
             rows = slice(16 * g, 16 * g + 16)
             p = p16[rows, cols]
             tiles = [
-                ext[2 * g : 2 * g + 2, :, pl.ds(base + LANES * t, LANES)].reshape(16, LANES) for t in range(9)
+                ext[2 * g : 2 * g + 2, :, base + LANES * t : base + LANES * (t + 1)].reshape(16, LANES) for t in range(9)
             ]
             total = None
             for off, near, beyond in ((0, w00, w10), (1, w01, w11)):
@@ -165,11 +192,16 @@
                     total = term if total is None else total + term
             adv[rows, cols] = total.astype(BF16)
 
+    def first_block(this_core, unit):
+        before = sum(BLOCKS[:unit]) % 4
+        right = (1 - this_core) if unit < HALF else this_core
+        return right * (4 + before) + (1 - right) * (4 - before - BLOCKS[unit])
+
     def columns(unit):
-        right = (1 - core) if unit < 2 else core
-        k = unit % 2
-        block = right * (4 + 2 * k) + (1 - right) * (2 - 2 * k)
-        return pl.ds(pl.multiple_of(block * LANES, 2 * LANES), 2 * LANES)
+        return pl.ds(pl.multiple_of(first_block(core, unit) * LANES, LANES), BLOCKS[unit] * LANES)
+
+    def rows_of(unit):
+        return pl.ds(STARTS[unit], BLOCKS[unit] * QUARTER)
 
     def remote(src, dst, send, recv, peer):
         return pltpu.make_async_remote_copy(
@@ -178,44 +210,50 @@
 
     def partial_copy(unit, hop):
         return remote(
-            part_tx.at[unit, hop], part_rx.at[unit, nlev - hop],
+            part_tx.at[hop, rows_of(unit)], part_rx.at[nlev - hop, rows_of(unit)],
             part_send.at[unit, hop], part_recv.at[unit, nlev - hop], lax.rem(me + hop, nlev),
         )
 
     def middle_copy(unit, owner, hop):
         return remote(
-            mid.at[unit, owner], mid.at[unit, owner], mid_send.at[unit, hop], mid_recv.at[unit, owner],
+            mid.at[owner, rows_of(unit)], mid.at[owner, rows_of(unit)], mid_send.at[unit, hop], mid_recv.at[unit, owner],
             lax.rem(owner + hop, nlev),
         )
 
-    def quarter(peer):
-        return pl.ds(pl.multiple_of(peer * QUARTER, QUARTER), QUARTER)
+    def quarter(unit, peer):
+        size = BLOCKS[unit] * QUARTER
+        return pl.ds(pl.multiple_of(first_block(core, unit) * LANES + peer * size, size), size)
+
+    def forward_on(this_core, unit):
+        first = first_block(this_core, unit)
+        for block in range(first, first + BLOCKS[unit]):
+            advect(block)
+        cols = slice(first * LANES, (first + BLOCKS[unit]) * LANES)
+        part[cols, :] = lax.dot_general(
+            adv[:, cols], w1[...], (((0,), (0,)), ((), ())), preferred_element_type=F32
+        )
 
     def forward(unit):
-        right = (1 - core) if unit < 2 else core
-        for i in (2 * (unit % 2), 2 * (unit % 2) + 1):
-            if unit >= 2:
-                halo_copy(1 - right, i).wait_recv()
-            elif i == 0:
-                halo_copy(1 - right, 0, 4).wait_recv()
-            advect(right * (4 + i) + (1 - right) * (3 - i))
-        part[unit] = lax.dot_general(
-            adv[:, columns(unit)], w1[...], (((0,), (0,)), ((), ())), preferred_element_type=F32
-        )
+        if unit == 0:
+            halo_copy(core, 0, 4).wait_recv()
+        elif unit >= HALF:
+            halo_copy(1 - core, sum(BLOCKS[HALF:unit]), BLOCKS[unit]).wait_recv()
+        pl.when(is_first)(functools.partial(forward_on, 0, unit))
+        pl.when(jnp.logical_not(is_first))(functools.partial(forward_on, 1, unit))
 
     def send_partial(unit):
         for hop in (2, 1, 3):
-            part_tx[unit, hop] = part[unit, quarter(lax.rem(me + hop, nlev)), :].astype(BF16)
+            part_tx[hop, rows_of(unit), :] = part[quarter(unit, lax.rem(me + hop, nlev)), :].astype(BF16)
             partial_copy(unit, hop).start()
 
     def complete(unit):
-        total = part[unit, quarter(me), :] + bf_v[...]
+        total = part[quarter(unit, me), :] + bf_v[...]
         for hop in (1, 3, 2):
             partial_copy(unit, hop).wait_recv()
-            total = total + part_rx[unit, nlev - hop].astype(F32)
+            total = total + part_rx[nlev - hop, rows_of(unit), :].astype(F32)
         first = silu(total).astype(BF16)
         second = jnp.dot(first, wm_v[...], preferred_element_type=F32) + bm_v[...]
-        mid[unit, me] = silu(second).astype(BF16)
+        mid[me, rows_of(unit), :] = silu(second).astype(BF16)
         for hop in (2, 1, 3):
             middle_copy(unit, me, hop).start()
 
@@ -223,11 +261,13 @@
         for hop in (1, 3, 2):
             middle_copy(unit, lax.rem(me + hop, nlev), nlev - hop).wait_recv()
         cols = columns(unit)
+        width = BLOCKS[unit] * LANES
         tendency = lax.dot_general(
-            w3[...], mid[unit].reshape(2 * LANES, w3.shape[1]), (((1,), (1,)), ((), ())), preferred_element_type=F32
+            w3[...], mid[:, rows_of(unit), :].reshape(width, w3.shape[1]), (((1,), (1,)), ((), ())),
+            preferred_element_type=F32,
         )
         updated = (adv[:, cols].astype(F32) + tendency).astype(BF16)
-        out[:, :, cols] = updated.reshape(levels, 8, 2 * LANES)
+        out[:, :, cols] = updated.reshape(levels, 8, width)
 
     forward(0)
 
@@ -241,25 +281,23 @@
         pl.semaphore_wait(lev_in, 1)
 
     send_partial(0)
-    forward(1)
-    send_partial(1)
-    pl.when(ahead)(send_slow)
-    forward(2)
-    send_partial(2)
-    forward(3)
-    send_partial(3)
-    for unit in range(4):
+    for unit in range(1, len(BLOCKS)):
+        if unit == HALF:
+            pl.when(ahead)(answer_west)
+        forward(unit)
+        send_partial(unit)
+    for unit in range(len(BLOCKS)):
         complete(unit)
-    for unit in range(4):
+    for unit in range(len(BLOCKS)):
         last(unit)
 
-    for unit in range(4):
+    for unit in range(len(BLOCKS)):
         for hop in range(1, nlev):
             partial_copy(unit, hop).wait_send()
             middle_copy(unit, me, hop).wait_send()
     halo_copy(1 - core, 0, 4).wait_send()
-    for i in range(4):
-        halo_copy(core, i).wait_send()
+    for i, tiles in ((0, 2), (2, 1), (3, 1)):
+        halo_copy(core, i, tiles).wait_send()
 
 
 def on_device(nband, nlev, fields, depart, fraction, w_first, b_first, w_middle, b_middle, w_last):
@@ -297,11 +335,11 @@
             V((nrow, ncols), BF16),
             V((nrow, hidden), BF16),
             V((nrow, hidden), BF16),
-            V((4, 2 * LANES, hidden), F32),
-            V((4, 4, QUARTER, hidden), BF16),
-            V((4, 4, QUARTER, hidden), BF16),
-            V((4, 4, QUARTER, hidden), BF16),
-            DMA((22,)), DMA((2, 4)), DMA((2, 4)), DMA((4, 4)), DMA((4, 4)), DMA((4, 4)), DMA((4, 4)),
+            V((ncols, hidden), F32),
+            V((4, ncols // 4, hidden), BF16),
+            V((4, ncols // 4, hidden), BF16),
+            V((4, ncols // 4, hidden), BF16),
+            DMA((22,)), DMA((2, 4)), DMA((2, 4)), DMA((5, 4)), DMA((5, 4)), DMA((5, 4)), DMA((5, 4)),
             pltpu.SemaphoreType.REGULAR, pltpu.SemaphoreType.REGULAR, pltpu.SemaphoreType.REGULAR,
         ],
         compiler_params=pltpu.CompilerParams(

time: 24 us -> 23.9 us (level)
  no operation moved by 1% of the time
where the time goes in v6:
time: 23.9 us; the launch traced here: 23.6 us
  Pallas kernels  22.8 us (95%)
  local copies, waits for them, and re-layouts  0.81 us (3%)
    pallas_call x1, Pallas kernels, on_device(): pl.pallas_call(functools.partial(kernel, nband, nlev), out_shape=jax.Shap...  22.8 us
    unnamed x1, local copies, waits for them, and re-layouts  0.81 us

profile of v6, /device:TPU:8, one launch (start us, length us, event | category | flops | bytes accessed | tf_op | source)
XLA Modules:
  0.0 23.6 jit_solution(7150739968346407886)
XLA Ops:
  0.0 22.8 %shard_map.82 = bf16[34,8,1024]{2,1,0:T(8,128)(2,1)S(1)} custom-call(bf16[34,8,1024]{2,1,0:T(8,128)(2,1)} %bitcast.8, s32[34,1024]{1,0:T(8,128)} %depart.1, bf16[34,2,1024]{2,1,0:T(2,128)(2,1)} %bitcast.11, bf16[1088,256]{1,0:T(8,128)(2,1)} %bitcast.9, bf16[1088,256]{1,0:T(8,128)(2,1)} %bitcast.10, bf16[256,256]{1,0:T(8,128)(2,1)} %w_middle.1, ...), custom_call_target="tpu_custom_call" | custom-call | tf_op jit(solution)/shard_map/pallas_call | solution.py:319
  22.8 0.8 %copy.10 = bf16[8,34,1024]{2,0,1:T(8,128)(2,1)} copy(bf16[8,34,1024]{2,0,1:T(8,128)(2,1)S(1)} %bitcast.7) | data formatting | bytes 1114112

commit v7 on v6

--- a/solution.py
+++ b/solution.py
@@ -134,8 +134,8 @@
         def _():
             tell(west_in, {"band": east})
 
+        halo_copy(1 - core, 0, 4).start()
         send_slow()
-        halo_copy(1 - core, 0, 4).start()
 
     pl.when(late)(start_loads)
 
@@ -144,7 +144,6 @@
         @pl.when(greeted)
         def _():
             pl.semaphore_wait(barrier, nlev + 1)
-            send_slow()
 
         @pl.when(ahead)
         def _():
@@ -153,6 +152,7 @@
         for peer in others:
             tell(peers_in, {"lev": peer})
         halo_copy(1 - core, 0, 4).start()
+        pl.when(greeted)(send_slow)
 
     loads[0].wait()
     loads[1].wait()

time: 23.9 us -> 23.9 us (level)
  no operation moved by 1% of the time
where the time goes in v7:
time: 23.9 us; the launch traced here: 23.6 us
  Pallas kernels  22.8 us (95%)
  local copies, waits for them, and re-layouts  0.81 us (3%)
    pallas_call x1, Pallas kernels, on_device(): pl.pallas_call(functools.partial(kernel, nband, nlev), out_shape=jax.Shap...  22.8 us
    unnamed x1, local copies, waits for them, and re-layouts  0.81 us

profile of v7, /device:TPU:8, one launch (start us, length us, event | category | flops | bytes accessed | tf_op | source)
XLA Modules:
  0.0 23.6 jit_solution(18329354085785515471)
XLA Ops:
  0.0 22.8 %shard_map.82 = bf16[34,8,1024]{2,1,0:T(8,128)(2,1)S(1)} custom-call(bf16[34,8,1024]{2,1,0:T(8,128)(2,1)} %bitcast.8, s32[34,1024]{1,0:T(8,128)} %depart.1, bf16[34,2,1024]{2,1,0:T(2,128)(2,1)} %bitcast.11, bf16[1088,256]{1,0:T(8,128)(2,1)} %bitcast.9, bf16[1088,256]{1,0:T(8,128)(2,1)} %bitcast.10, bf16[256,256]{1,0:T(8,128)(2,1)} %w_middle.1, ...), custom_call_target="tpu_custom_call" | custom-call | tf_op jit(solution)/shard_map/pallas_call | solution.py:319
  22.8 0.8 %copy.10 = bf16[8,34,1024]{2,0,1:T(8,128)(2,1)} copy(bf16[8,34,1024]{2,0,1:T(8,128)(2,1)S(1)} %bitcast.7) | data formatting | bytes 1114112
